TPU v7x, 256 devices: a whole 4x4x8 slice. The times are simulated.
256 devices in a mesh: leaf: 64 (over x, z, core), vec: 4 (over y).
Axes of the slice: x: 4, y: 4, z: 8, core: 2. Of those that a mesh axis runs over, the one named last changes fastest.
Arguments:
- panels: float32 [32, 524288], P('vec', 'leaf'), may hold values from -6 to 6
- near_tiles: float32 [4096, 4, 128, 128], P('leaf', None, 'vec'), may hold values from -0.25 to 0.25
- near_cols: int32 [4096, 4], P('leaf'), may hold values from 0 to 4095, as said below
- leaf_order: int32 [4096, 128], P('leaf'), may hold values from 0 to 127, each once within a row
- leaf_basis: float32 [4096, 64, 128], P('leaf'), may hold values from -0.5 to 0.5
- local_mats: float32 [64, 63, 64, 128], P('leaf'), may hold values from -0.75 to 0.75
- local_flags: int32 [64, 63], P('leaf'), may hold values 0 or 1
- cross_coupling: float32 [62, 64, 64], replicated, may hold values from -0.75 to 0.75
- cross_transfer: float32 [60, 64, 64], replicated, may hold values from -0.75 to 0.75
- cross_flags: int32 [62], replicated, may hold values 0 or 1
Outputs:
- product: float32 [32, 524288], P('vec', 'leaf')
Inputs may be any that keep to these rules, and one draw needn't show every extreme that they name: `near_cols`: every entry of row i names a leaf within 8 leaves of leaf i. `leaf_order`: each row is a permutation of 0 to 127.
All inputs are finite; a program needn't handle non-finite values. No bound on the sum of `local_flags` on one device may be relied on, other than what follows from the above.
Results may differ from a plain program's by a relative error of at most 0.00022.
Values sent between devices are 32-bit elements; how exact they have to be, the bound alone decides.
No kernel may reach another device: no remote copies, remote signals or barrier semaphores. Data moves between devices by JAX's collectives and lax.ppermute only.
A program may use at most 64 MiB of HBM per device.

v0:
```python
import math

import jax
import jax.numpy as jnp
from jax import lax
from jax.sharding import PartitionSpec as P

W = 8


precise = lax.Precision.HIGHEST
root_half = 1.0 / math.sqrt(2.0)


def extended_2(cells, sides, width):
    for axis, dim in sides:
        count = lax.axis_size(axis)
        ends = count - 1
        head = lax.slice_in_dim(cells, 0, width, axis=dim)
        tail = lax.slice_in_dim(cells, cells.shape[dim] - width, cells.shape[dim], axis=dim)
        cells = jnp.concatenate(
            [
                lax.ppermute(tail, axis, [(i, (i + 1) % count) for i in range(ends)]),
                cells,
                lax.ppermute(head, axis, [((i + 1) % count, i) for i in range(ends)]),
            ],
            axis=dim,
        )
    return cells


def partner(block, axis, bit):
    count = lax.axis_size(axis)
    route = []
    for low in range(count):
        high = low | 1 << bit
        if high != low and high < count:
            route += [(low, high), (high, low)]
    return lax.ppermute(block, axis, route)


def near_product(tile_rows, sources):
    return jnp.einsum("lnqp,slnp->slq", tile_rows, sources, precision=precise)


def local(
    panels,
    near_tiles,
    near_cols,
    leaf_order,
    leaf_basis,
    local_mats,
    local_flags,
    cross_coupling,
    cross_transfer,
    cross_flags,
):
    rhs_dev = panels.shape[0]
    leaves = leaf_basis.shape[0]
    skel_rank = leaf_basis.shape[1]
    leaf_size = leaf_basis.shape[2]
    halo_cells = W * leaf_size
    leaf_count = lax.axis_size("leaf")
    leaf_index = lax.axis_index("leaf")
    cross_depth = leaf_count.bit_length() - 1
    places = jnp.arange(leaf_size, dtype=jnp.int32)
    order_hot = (leaf_order[:, :, None] == places[None, None, :]).astype(jnp.float32)
    ordered = jnp.einsum(
        "lpm,slm->slp", order_hot, panels.reshape(rhs_dev, leaves, leaf_size), precision=precise
    )
    ordered_flat = ordered.reshape(rhs_dev, leaves * leaf_size)
    local_cols = near_cols - leaf_index * leaves + W
    rim_leaves = jnp.arange(leaves + 2 * W, dtype=jnp.int32)
    select_hot = (local_cols[:, :, None] == rim_leaves[None, None, :]).astype(jnp.float32)
    rimmed = extended_2(ordered_flat, (("leaf", 1),), halo_cells)
    extended = lax.all_gather(rimmed, "vec", axis=0, tiled=True)
    blocked = extended.reshape(extended.shape[0], leaves + 2 * W, leaf_size)
    partial_rows = near_product(
        near_tiles, jnp.einsum("lne,sep->slnp", select_hot, blocked, precision=precise)
    )
    near_field = lax.all_to_all(partial_rows, "vec", split_axis=0, concat_axis=2, tiled=True)
    local_blocks = local_mats[0]
    local_admit = local_flags[0].astype(jnp.float32)
    leaf_skel = jnp.einsum("lkp,slp->lsk", leaf_basis, ordered, precision=precise)
    skeleton = leaf_skel.reshape(leaves // 2, 2, rhs_dev, skel_rank).sum(axis=1) * root_half
    local_depth = leaves.bit_length() - 1
    coupled = []
    for tree_level in range(1, local_depth):
        node_count = leaves >> tree_level
        first_node = leaves - (leaves >> tree_level - 1)
        blocks = local_blocks[first_node : first_node + node_count]
        sibling = skeleton.reshape(node_count // 2, 2, rhs_dev, skel_rank)[:, ::-1].reshape(
            skeleton.shape
        )
        term = jnp.einsum("jkm,jsm->jsk", blocks[:, :, :skel_rank], sibling, precision=precise)
        coupled.append(local_admit[first_node : first_node + node_count, None, None] * term)
        lifted = jnp.einsum("jsk,jkm->jsm", skeleton, blocks[:, :, skel_rank:], precision=precise)
        skeleton = lifted.reshape(node_count // 2, 2, rhs_dev, skel_rank).sum(axis=1) * root_half
    device_block = local_blocks[leaves - 2]
    device_skel = skeleton[0]
    device_lift = jnp.dot(device_skel, device_block[:, skel_rank:], precision=precise)

    def cross_index(level_bit):
        return leaf_count - (leaf_count >> level_bit - 1) + (leaf_index >> level_bit)

    def transfer_at(level_bit):
        if level_bit == 0:
            return device_block[:, skel_rank:]
        return lax.dynamic_index_in_dim(cross_transfer, cross_index(level_bit), 0, keepdims=False)

    cross_terms = []
    current, carried = (device_skel, device_lift)
    for level_bit in range(cross_depth):
        sibling_skel, sibling_up = partner((current, carried), "leaf", level_bit)
        if level_bit == 0:
            coupling = device_block[:, :skel_rank]
            admitted = local_admit[leaves - 2]
        else:
            node_index = cross_index(level_bit)
            coupling = lax.dynamic_index_in_dim(cross_coupling, node_index, 0, keepdims=False)
            admitted = lax.dynamic_index_in_dim(cross_flags, node_index, 0, keepdims=False).astype(
                jnp.float32
            )
        cross_terms.append(admitted * jnp.dot(sibling_skel, coupling.T, precision=precise))
        if level_bit < cross_depth - 1:
            current = (carried + sibling_up) * root_half
            if level_bit + 1 <= cross_depth - 2:
                carried = jnp.dot(current, transfer_at(level_bit + 1), precision=precise)
    downward = cross_terms[cross_depth - 1]
    for level_bit in range(cross_depth - 2, -1, -1):
        downward = cross_terms[level_bit] + jnp.dot(
            downward, transfer_at(level_bit).T, precision=precise
        )
    downward = downward[None]
    for tree_level in range(local_depth - 1, 0, -1):
        node_count = leaves >> tree_level
        first_node = leaves - (leaves >> tree_level - 1)
        transfer = local_blocks[first_node : first_node + node_count, :, skel_rank:]
        spread = jnp.repeat(downward, 2, axis=0)
        downward = coupled[tree_level - 1] + jnp.einsum(
            "jkm,jsm->jsk", transfer, spread, precision=precise
        )
    far_field = jnp.einsum(
        "lkp,lsk->slp", leaf_basis, jnp.repeat(downward, 2, axis=0), precision=precise
    )
    combined = near_field + far_field
    restored = jnp.einsum("lpm,slp->slm", order_hot, combined, precision=precise)
    return restored.reshape(rhs_dev, leaves * leaf_size)


def solution(mesh):
    return jax.shard_map(
        local,
        mesh=mesh,
        in_specs=(
            P("vec", "leaf"),
            P("leaf", None, "vec", None),
            P("leaf", None),
            P("leaf", None),
            P("leaf", None, None),
            P("leaf", None, None, None),
            P("leaf", None),
            P(),
            P(),
            P(),
        ),
        out_specs=P("vec", "leaf"),
        check_vma=False,
    )
```

profile of v0, /device:TPU:2, one launch (start us, length us, event | category | flops | bytes accessed | tf_op | source)
XLA Modules:
  0.0 147.3 jit_solution(17672255589583343882)
XLA Ops:
  6.5 1.4 slice_bitcast_fusion
  8.0 1.1 slice_bitcast_fusion.1
  9.1 1.0 slice_bitcast_fusion.2
  10.1 0.9 slice_bitcast_fusion.3
  11.0 0.8 slice_bitcast_fusion.4
  11.8 4.7 %fusion.2 = f32[64,128,8]{1,2,0:T(8,128)S(1)} fusion(s32[64,128]{1,0:T(8,128)S(1)} %copy-done.5, f32[8,8192]{1,0:T(8,128)S(1)} %copy-done.4), kind=kOutput, calls=%fused_computation.4 | convolution fusion | flops 101711872 | bytes 557056 | tf_op jit(solution)/shard_map/lpm,slm->slp/dot_general | solution.py:68
  16.6 3.4 %bitcast_reduce_fusion = f32[32,8,64]{2,1,0:T(8,128)S(1)} fusion(f32[64,64,128]{2,1,0:T(8,128)S(1)} %copy-done, f32[64,128,8]{1,2,0:T(8,128)S(1)} %fusion.2), kind=kOutput, calls=%fused_computation.50 | convolution fusion | flops 50348032 | bytes 2424832 | tf_op jit(solution)/shard_map/lkp,slp->lsk/dot_general | solution.py:84
  20.0 1.2 bitcast_reduce_fusion.1
  21.1 0.7 bitcast_reduce_fusion.2
  21.8 0.4 bitcast_reduce_fusion.3
  22.2 0.3 bitcast_reduce_fusion.4
  22.8 0.8 slice_bitcast_fusion.5
  23.8 0.5 collective-permute-start.3
  24.3 1.9 %collective-permute-start = (f32[8,1024]{1,0:T(8,128)S(1)}, f32[8,1024]{1,0:T(8,128)S(1)}, u32[]{:S(2)}, u32[]{:S(2)}) collective-permute-start(f32[8,1024]{1,0:T(8,128)S(1)} %get-tuple-element.5), channel_id=1, source_target_pairs={{0,4},{4,8},{8,12},{12,16},{16,20},{20,24},{24,28},{28,32},{32,36}... | collective-permute-start | bytes 98312 | tf_op jit(solution)/shard_map/ppermute | solution.py:23
  26.2 7.4 %collective-permute-start.1 = (f32[8,1024]{1,0:T(8,128)S(1)}, f32[8,1024]{1,0:T(8,128)S(1)}, u32[]{:S(2)}, u32[]{:S(2)}) collective-permute-start(f32[8,1024]{1,0:T(8,128)S(1)} %get-tuple-element.6), channel_id=1, source_target_pairs={{4,0},{8,4},{12,8},{16,12},{20,16},{24,20},{28,24},{32,28},{36,32}... | collective-permute-start | bytes 98312 | tf_op jit(solution)/shard_map/ppermute | solution.py:25
  33.8 0.5 convolution_multiply_fusion.2
  34.3 0.9 convolution_multiply_fusion.1
  35.2 1.8 %convolution_multiply_fusion = f32[32,8,64]{2,1,0:T(8,128)S(1)} fusion(f32[32,8,64]{2,1,0:T(8,128)S(1)} %bitcast.176, f32[32,64,128]{2,1,0:T(8,128)S(1)} %slice_bitcast_fusion, f32[32]{0:T(128)S(1)} %slice_bitcast_fusion.10), kind=kOutput, calls=%fused_computation.13 | convolution fusion | flops 12599296 | bytes 1179776 | tf_op jit(solution)/shard_map/jkm,jsm->jsk/dot_general | solution.py:95
  37.1 0.9 fusion.73
  38.0 3.6 %collective-permute-done.5 = f32[8,64]{1,0:T(8,128)S(1)} collective-permute-done((f32[8,64]{1,0:T(8,128)S(1)}, f32[8,64]{1,0:T(8,128)S(1)}, u32[]{:S(2)}, u32[]{:S(2)}) %collective-permute-start.5) | collective-permute-done | bytes 2080 | tf_op jit(solution)/shard_map/ppermute | solution.py:39
  41.6 0.9 fusion.68
  42.8 4.2 %collective-permute-done.7 = f32[8,64]{1,0:T(8,128)S(1)} collective-permute-done((f32[8,64]{1,0:T(8,128)S(1)}, f32[8,64]{1,0:T(8,128)S(1)}, u32[]{:S(2)}, u32[]{:S(2)}) %collective-permute-start.7) | collective-permute-done | bytes 2080 | tf_op jit(solution)/shard_map/ppermute | solution.py:39
  47.0 0.9 fusion.63
  47.9 4.7 %collective-permute-start.9 = (f32[8,64]{1,0:T(8,128)S(1)}, f32[8,64]{1,0:T(8,128)S(1)}, u32[]{:S(2)}, u32[]{:S(2)}) collective-permute-start(f32[8,64]{1,0:T(8,128)S(1)} %fusion.63), channel_id=1, source_target_pairs={{0,32},{32,0},{4,36},{36,4},{8,40},{40,8},{12,44},{44,12},{16,48},... | collective-permute-start | bytes 6152 | tf_op jit(solution)/shard_map/ppermute | solution.py:39
  52.7 2.8 %collective-permute-done.9 = f32[8,64]{1,0:T(8,128)S(1)} collective-permute-done((f32[8,64]{1,0:T(8,128)S(1)}, f32[8,64]{1,0:T(8,128)S(1)}, u32[]{:S(2)}, u32[]{:S(2)}) %collective-permute-start.9) | collective-permute-done | bytes 2080 | tf_op jit(solution)/shard_map/ppermute | solution.py:39
  55.4 0.9 fusion.58
  56.5 3.4 %collective-permute-done.11 = f32[8,64]{1,0:T(8,128)S(1)} collective-permute-done((f32[8,64]{1,0:T(8,128)S(1)}, f32[8,64]{1,0:T(8,128)S(1)}, u32[]{:S(2)}, u32[]{:S(2)}) %collective-permute-start.11) | collective-permute-done | bytes 2080 | tf_op jit(solution)/shard_map/ppermute | solution.py:39
  59.9 2.4 %collective-permute-start.12 = (f32[8,64]{1,0:T(8,128)S(1)}, f32[8,64]{1,0:T(8,128)S(1)}, u32[]{:S(2)}, u32[]{:S(2)}) collective-permute-start(f32[8,64]{1,0:T(8,128)S(1)} %add_multiply_fusion), channel_id=1, source_target_pairs={{0,128},{128,0},{4,132},{132,4},{8,136},{136,8},{12,140},{140,12},... | collective-permute-start | bytes 6152 | tf_op jit(solution)/shard_map/ppermute | solution.py:39
  62.4 0.7 slice.157
  63.0 0.7 fusion.131
  67.1 1.2 collective-permute-start.10
  68.3 0.9 convolution_multiply_fusion.5
  69.2 0.9 fusion.56
  70.1 0.6 collective-permute-done.10
  70.8 4.4 %collective-permute-start.8 = (f32[8,64]{1,0:T(8,128)S(1)}, f32[8,64]{1,0:T(8,128)S(1)}, u32[]{:S(2)}, u32[]{:S(2)}) collective-permute-start(f32[8,64]{1,0:T(8,128)S(1)} %add_multiply_fusion.2), channel_id=1, source_target_pairs={{0,32},{32,0},{4,36},{36,4},{8,40},{40,8},{12,44},{44,12},{16,48},... | collective-permute-start | bytes 6152 | tf_op jit(solution)/shard_map/ppermute | solution.py:39
  75.2 0.9 fusion.10
  76.1 0.9 fusion.61
  77.0 1.3 collective-permute-done.8
  78.3 1.1 collective-permute-start.6
  79.4 0.9 fusion.11
  80.3 0.9 fusion.66
  81.2 0.8 pad_maximum_fusion
  82.0 0.8 collective-permute-done.6
  82.8 0.9 fusion.12
  83.7 0.9 fusion.71
  84.6 0.9 fusion.13
  85.8 0.9 fusion.14
  86.7 1.1 convolution_add_fusion.4
  87.8 1.3 convolution_add_fusion.3
  89.1 1.5 %convolution_add_fusion.2 = f32[8,8,64]{2,1,0:T(8,128)S(1)} fusion(f32[8,8,64]{2,1,0:T(8,128)S(1)} %convolution_multiply_fusion.2, f32[8,8,64]{2,1,0:T(8,128)S(1)} %bitcast.183, f32[63,64,128]{2,1,0:T(8,128)} %bitcast.163), kind=kOutput, calls=%fused_computation.16 | convolution fusion | flops 3149824 | bytes 311296 | tf_op jit(solution)/shard_map/jkm,jsm->jsk/dot_general | solution.py:140
  90.7 2.0 %convolution_add_fusion.1 = f32[16,8,64]{2,1,0:T(8,128)S(1)} fusion(f32[16,8,64]{2,1,0:T(8,128)S(1)} %convolution_multiply_fusion.1, f32[16,8,64]{2,1,0:T(8,128)S(1)} %bitcast.180, f32[63,64,128]{2,1,0:T(8,128)} %bitcast.164), kind=kOutput, calls=%fused_computation.14 | convolution fusion | flops 6299648 | bytes 622592 | tf_op jit(solution)/shard_map/jkm,jsm->jsk/dot_general | solution.py:140
  92.7 16.2 %all-gather.2.cloned.1.call-done = f32[32,10240]{1,0:T(8,128)} async-done(((f32[8,10240]{1,0:T(8,128)}), f32[32,10240]{1,0:T(8,128)}) %all-gather.2.cloned.1.call-update) | async-done | bytes 1310736 | tf_op jit(solution)/shard_map/all_gather | solution.py:76
  108.9 1.5 %copy.22 = f32[4,8,80,128]{3,2,1,0:T(8,128)S(1)} copy(f32[4,8,80,128]{3,1,2,0:T(8,128)} %bitcast.172) | data formatting | bytes 2621440
  110.5 1.9 %convolution_bitcast_fusion.1 = f32[32,64,4,128]{3,1,2,0:T(8,128)S(1)} fusion(f32[32,80,128,1]{2,1,0,3:T(8,128)S(1)} %bitcast.166, s32[64,4]{0,1:T(4,128)S(1)} %subtract_add_fusion), kind=kOutput, calls=%fused_computation.5 | convolution fusion | flops 1006653440 | bytes 5506048 | tf_op jit(solution)/shard_map/lne,sep->slnp/dot_general | solution.py:79
  112.7 6.2 %fusion.5 = f32[32,64,32]{2,0,1:T(8,128)S(1)} fusion(f32[64,4,32,128]{3,2,1,0:T(8,128)S(1)} %copy-done.1, f32[32,64,4,128]{3,1,2,0:T(8,128)S(1)} %convolution_bitcast_fusion.1), kind=kOutput, calls=%fused_computation.8 | convolution fusion | flops 402653184 | bytes 8650752 | tf_op jit(solution)/shard_map/lnqp,slnp->slq/dot_general | solution.py:43
  118.9 1.4 copy.17
  120.3 2.1 %reshape.133 = f32[4,1,16384]{2,1,0:T(1,128)} reshape(f32[32,32,64]{2,1,0:T(8,128)} %bitcast.167) | data formatting | bytes 524288
  122.4 3.6 %all-to-all-start = ((f32[4,1,16384]{2,1,0:T(1,128)}), f32[4,1,16384]{2,1,0:T(1,128)S(1)}, u32[]{:S(2)}, u32[]{:S(2)}) async-start(f32[4,1,16384]{2,1,0:T(1,128)} %reshape.133), calls=%async_computation | async-start | bytes 524288 | tf_op jit(solution)/shard_map/all_to_all | solution.py:81
  126.0 3.0 %convolution_add_fusion = f32[32,8,64]{2,1,0:T(8,128)S(1)} fusion(f32[32,8,64]{2,1,0:T(8,128)S(1)} %convolution_multiply_fusion, f32[32,8,64]{2,1,0:T(8,128)S(1)} %bitcast.177, f32[63,64,128]{2,1,0:T(8,128)} %bitcast.165), kind=kOutput, calls=%fused_computation.12 | convolution fusion | flops 12599296 | bytes 1245184 | tf_op jit(solution)/shard_map/jkm,jsm->jsk/dot_general | solution.py:140
  129.1 3.5 %all-to-all-done = f32[4,1,16384]{2,1,0:T(1,128)S(1)} async-done(((f32[4,1,16384]{2,1,0:T(1,128)}), f32[4,1,16384]{2,1,0:T(1,128)S(1)}, u32[]{:S(2)}, u32[]{:S(2)}) %all-to-all-start) | async-done | bytes 262176 | tf_op jit(solution)/shard_map/all_to_all | solution.py:81
  132.6 0.5 broadcast.17
  133.1 1.4 reduce.2
  135.1 1.9 %fusion.9 = f32[8,64,128]{2,0,1:T(8,128)S(1)} fusion(f32[8,64,128]{2,0,1:T(8,128)S(1)} %copy.19, f32[64,8,64]{2,1,0:T(8,128)S(1)} %bitcast.174, f32[64,64,128]{2,1,0:T(8,128)S(1)} %copy-done), kind=kOutput, calls=%fused_computation.11 | convolution fusion | flops 50397184 | bytes 2752512 | tf_op jit(solution)/shard_map/lkp,lsk->slp/dot_general | solution.py:143
  136.9 3.6 %convolution_bitcast_fusion = f32[8,8192]{1,0:T(8,128)} fusion(f32[8,64,128]{2,0,1:T(8,128)S(1)} %fusion.9, s32[64,128]{1,0:T(8,128)S(1)} %copy-done.5), kind=kOutput, calls=%fused_computation | convolution fusion | flops 101711872 | bytes 557056 | tf_op jit(solution)/shard_map/lpm,slp->slm/dot_general | solution.py:147
  (58 shorter events, 2.8 us)
Async XLA Ops:
  6.5 10.1 %copy-start = (f32[64,64,128]{2,1,0:T(8,128)S(1)}, f32[64,64,128]{2,1,0:T(8,128)}, u32[]{:S(2)}) copy-start(f32[64,64,128]{2,1,0:T(8,128)} %param.14) | copy-start | bytes 6291460
  6.5 5.3 %copy-start.4 = (f32[8,8192]{1,0:T(8,128)S(1)}, f32[8,8192]{1,0:T(8,128)}, u32[]{:S(2)}) copy-start(f32[8,8192]{1,0:T(8,128)} %param.10) | copy-start | bytes 786436
  6.5 5.3 %copy-start.5 = (s32[64,128]{1,0:T(8,128)S(1)}, s32[64,128]{1,0:T(8,128)}, u32[]{:S(2)}) copy-start(s32[64,128]{1,0:T(8,128)} %param.13) | copy-start | bytes 98308
  6.5 102.4 %all-gather.2.cloned.1.call-start = ((), (), s32[]{:S(2)}) async-start(), calls=%async_computation.1 | async-start | bytes 1638400 | tf_op jit(solution)/shard_map/all_gather | solution.py:76
  16.6 17.0 %copy-start.6 = (s32[1,63]{1,0:T(1,128)S(1)}, s32[1,63]{1,0:T(1,128)}, u32[]{:S(2)}) copy-start(s32[1,63]{1,0:T(1,128)} %param.16) | copy-start | bytes 760
  21.8 40.6 %copy-start.3 = (s32[64,4]{0,1:T(4,128)S(1)}, s32[64,4]{0,1:T(4,128)}, u32[]{:S(2)}) copy-start(s32[64,4]{0,1:T(4,128)} %param.12) | copy-start | bytes 3076
  21.8 41.2 %copy-start.2 = (s32[62]{0:T(128)S(1)}, s32[62]{0:T(128)}, u32[]{:S(2)}) copy-start(s32[62]{0:T(128)} %param.19) | copy-start | bytes 748
  22.8 63.0 %collective-permute-start.2 = (f32[8,64]{1,0:T(8,128)S(1)}, f32[8,64]{1,0:T(8,128)S(1)}, u32[]{:S(2)}, u32[]{:S(2)}) collective-permute-start(f32[8,64]{1,0:T(8,128)S(1)} %fusion.15), channel_id=1, source_target_pairs={{0,4},{4,0},{8,12},{12,8},{16,20},{20,16},{24,28},{28,24},{32,36},... | collective-permute-start | bytes 6152 | tf_op jit(solution)/shard_map/ppermute | solution.py:39
  23.8 13.3 %collective-permute-start.3 = (f32[8,64]{1,0:T(8,128)S(1)}, f32[8,64]{1,0:T(8,128)S(1)}, u32[]{:S(2)}, u32[]{:S(2)}) collective-permute-start(f32[8,64]{1,0:T(8,128)S(1)} %fusion.89), channel_id=1, source_target_pairs={{0,4},{4,0},{8,12},{12,8},{16,20},{20,16},{24,28},{28,24},{32,36},... | collective-permute-start | bytes 6152 | tf_op jit(solution)/shard_map/ppermute | solution.py:39
  24.3 56.9 %collective-permute-start = (f32[8,1024]{1,0:T(8,128)S(1)}, f32[8,1024]{1,0:T(8,128)S(1)}, u32[]{:S(2)}, u32[]{:S(2)}) collective-permute-start(f32[8,1024]{1,0:T(8,128)S(1)} %get-tuple-element.5), channel_id=1, source_target_pairs={{0,4},{4,8},{8,12},{12,16},{16,20},{20,24},{24,28},{28,32},{32,36}... | collective-permute-start | bytes 98312 | tf_op jit(solution)/shard_map/ppermute | solution.py:23
  26.2 55.0 %collective-permute-start.1 = (f32[8,1024]{1,0:T(8,128)S(1)}, f32[8,1024]{1,0:T(8,128)S(1)}, u32[]{:S(2)}, u32[]{:S(2)}) collective-permute-start(f32[8,1024]{1,0:T(8,128)S(1)} %get-tuple-element.6), channel_id=1, source_target_pairs={{4,0},{8,4},{12,8},{16,12},{20,16},{24,20},{28,24},{32,28},{36,32}... | collective-permute-start | bytes 98312 | tf_op jit(solution)/shard_map/ppermute | solution.py:25
  38.0 3.6 %collective-permute-start.5 = (f32[8,64]{1,0:T(8,128)S(1)}, f32[8,64]{1,0:T(8,128)S(1)}, u32[]{:S(2)}, u32[]{:S(2)}) collective-permute-start(f32[8,64]{1,0:T(8,128)S(1)} %fusion.73), channel_id=1, source_target_pairs={{0,8},{8,0},{4,12},{12,4},{16,24},{24,16},{20,28},{28,20},{32,40},... | collective-permute-start | bytes 6152 | tf_op jit(solution)/shard_map/ppermute | solution.py:39
  42.5 4.5 %collective-permute-start.7 = (f32[8,64]{1,0:T(8,128)S(1)}, f32[8,64]{1,0:T(8,128)S(1)}, u32[]{:S(2)}, u32[]{:S(2)}) collective-permute-start(f32[8,64]{1,0:T(8,128)S(1)} %fusion.68), channel_id=1, source_target_pairs={{0,16},{16,0},{4,20},{20,4},{8,24},{24,8},{12,28},{28,12},{32,48},... | collective-permute-start | bytes 6152 | tf_op jit(solution)/shard_map/ppermute | solution.py:39
  47.9 7.5 %collective-permute-start.9 = (f32[8,64]{1,0:T(8,128)S(1)}, f32[8,64]{1,0:T(8,128)S(1)}, u32[]{:S(2)}, u32[]{:S(2)}) collective-permute-start(f32[8,64]{1,0:T(8,128)S(1)} %fusion.63), channel_id=1, source_target_pairs={{0,32},{32,0},{4,36},{36,4},{8,40},{40,8},{12,44},{44,12},{16,48},... | collective-permute-start | bytes 6152 | tf_op jit(solution)/shard_map/ppermute | solution.py:39
  56.3 3.6 %collective-permute-start.11 = (f32[8,64]{1,0:T(8,128)S(1)}, f32[8,64]{1,0:T(8,128)S(1)}, u32[]{:S(2)}, u32[]{:S(2)}) collective-permute-start(f32[8,64]{1,0:T(8,128)S(1)} %fusion.58), channel_id=1, source_target_pairs={{0,64},{64,0},{4,68},{68,4},{8,72},{72,8},{12,76},{76,12},{16,80},... | collective-permute-start | bytes 6152 | tf_op jit(solution)/shard_map/ppermute | solution.py:39
  59.9 7.1 %collective-permute-start.12 = (f32[8,64]{1,0:T(8,128)S(1)}, f32[8,64]{1,0:T(8,128)S(1)}, u32[]{:S(2)}, u32[]{:S(2)}) collective-permute-start(f32[8,64]{1,0:T(8,128)S(1)} %add_multiply_fusion), channel_id=1, source_target_pairs={{0,128},{128,0},{4,132},{132,4},{8,136},{136,8},{12,140},{140,12},... | collective-permute-start | bytes 6152 | tf_op jit(solution)/shard_map/ppermute | solution.py:39
  66.8 17.8 %collective-permute-start.4 = (f32[8,64]{1,0:T(8,128)S(1)}, f32[8,64]{1,0:T(8,128)S(1)}, u32[]{:S(2)}, u32[]{:S(2)}) collective-permute-start(f32[8,64]{1,0:T(8,128)S(1)} %add_multiply_fusion.4), channel_id=1, source_target_pairs={{0,8},{8,0},{4,12},{12,4},{16,24},{24,16},{20,28},{28,20},{32,40},... | collective-permute-start | bytes 6152 | tf_op jit(solution)/shard_map/ppermute | solution.py:39
  67.1 3.7 %collective-permute-start.10 = (f32[8,64]{1,0:T(8,128)S(1)}, f32[8,64]{1,0:T(8,128)S(1)}, u32[]{:S(2)}, u32[]{:S(2)}) collective-permute-start(f32[8,64]{1,0:T(8,128)S(1)} %add_multiply_fusion.1), channel_id=1, source_target_pairs={{0,64},{64,0},{4,68},{68,4},{8,72},{72,8},{12,76},{76,12},{16,80},... | collective-permute-start | bytes 6152 | tf_op jit(solution)/shard_map/ppermute | solution.py:39
  70.8 7.5 %collective-permute-start.8 = (f32[8,64]{1,0:T(8,128)S(1)}, f32[8,64]{1,0:T(8,128)S(1)}, u32[]{:S(2)}, u32[]{:S(2)}) collective-permute-start(f32[8,64]{1,0:T(8,128)S(1)} %add_multiply_fusion.2), channel_id=1, source_target_pairs={{0,32},{32,0},{4,36},{36,4},{8,40},{40,8},{12,44},{44,12},{16,48},... | collective-permute-start | bytes 6152 | tf_op jit(solution)/shard_map/ppermute | solution.py:39
  78.3 4.5 %collective-permute-start.6 = (f32[8,64]{1,0:T(8,128)S(1)}, f32[8,64]{1,0:T(8,128)S(1)}, u32[]{:S(2)}, u32[]{:S(2)}) collective-permute-start(f32[8,64]{1,0:T(8,128)S(1)} %add_multiply_fusion.3), channel_id=1, source_target_pairs={{0,16},{16,0},{4,20},{20,4},{8,24},{24,8},{12,28},{28,12},{32,48},... | collective-permute-start | bytes 6152 | tf_op jit(solution)/shard_map/ppermute | solution.py:39
  110.5 2.2 %copy-start.1 = (f32[64,4,32,128]{3,2,1,0:T(8,128)S(1)}, f32[64,4,32,128]{3,2,1,0:T(8,128)}, u32[]{:S(2)}) copy-start(f32[64,4,32,128]{3,2,1,0:T(8,128)} %param.11) | copy-start | bytes 12582916
  122.4 10.2 %all-to-all-start = ((f32[4,1,16384]{2,1,0:T(1,128)}), f32[4,1,16384]{2,1,0:T(1,128)S(1)}, u32[]{:S(2)}, u32[]{:S(2)}) async-start(f32[4,1,16384]{2,1,0:T(1,128)} %reshape.133), calls=%async_computation | async-start | bytes 524288 | tf_op jit(solution)/shard_map/all_to_all | solution.py:81
Sparse Core Ops, SparseCore 0:
  82.1 26.7 all-gather.1
where the time goes:
time: 149 us; the launch traced here: 147 us
  matrix products  50.3 us (34%)
  waiting for transfers between devices  36.5 us (24%)
  starting transfers between devices  27.5 us (18%)
  between operations  16.7 us (11%)
  local copies, waits for them, and re-layouts  14.1 us (9%)
  other arithmetic  2.19 us (1%)
    ppermute x11, waiting for transfers between devices, partner(): return lax.ppermute(block, axis, route)  16.7 us
    all_gather x1, waiting for transfers between devices, local(): extended = lax.all_gather(rimmed, 'vec', axis=0, tiled=True)  16.2 us
    ppermute x11, starting transfers between devices, partner(): return lax.ppermute(block, axis, route)  14.6 us
    dot_general x5, matrix products, local(): jnp.einsum('jkm,jsm->jsk', transfer, spread, precision=precise)  9.07 us
    ppermute x1, starting transfers between devices, extended_2(): lax.ppermute(head, axis, [((i + 1) % count, i) for i in range(ends)])  7.35 us
    dot_general x1, matrix products, near_product(): return jnp.einsum('lnqp,slnp->slq', tile_rows, sources, precision=precise)  6.22 us
    dot_general x6, matrix products, local(): jnp.dot(sibling_skel, coupling.T, precision=precise)  5.39 us
    slice x5, local copies, waits for them, and re-layouts, local(): blocks = local_blocks[first_node:first_node + node_count]  5.26 us
  transfers between devices with their start and end apart: 15, of which 9 were waited for; matrix products, arithmetic and copies ran while one was open for 20% of the time, Pallas kernels for 0%

commit v1 on v0

v1 whole, which is shorter than its diff:
```python
import math

import jax
import jax.numpy as jnp
from jax import lax
from jax.experimental import pallas as pl
from jax.experimental.pallas import tpu as pltpu
from jax.sharding import PartitionSpec as P

W = 8
ROOT_HALF = 1.0 / math.sqrt(2.0)
F32, BF16 = jnp.float32, jnp.bfloat16
NN = (((1,), (0,)), ((), ()))
NT = (((1,), (1,)), ((), ()))


def params():
    return pltpu.CompilerParams(vmem_limit_bytes=48 * 1024 * 1024)


def vmem():
    return pl.BlockSpec(memory_space=pltpu.VMEM)


def smem():
    return pl.BlockSpec(memory_space=pltpu.SMEM)


def halves(x):
    hi = x.astype(BF16).astype(F32)
    return hi, x - hi


def left_rows(x):
    hi, lo = halves(x)
    rows = jnp.concatenate([hi, lo], axis=0).astype(BF16)
    return jnp.concatenate([rows, rows], axis=1)


def mul_nn(x, w):
    m = x.shape[0]
    hi, lo = halves(w)
    both = jnp.concatenate([hi.astype(BF16), lo.astype(BF16)], axis=0)
    d = lax.dot_general(left_rows(x), both, NN, preferred_element_type=F32)
    return d[:m] + d[m:]


def mul_nt(x, w):
    m = x.shape[0]
    hi, lo = halves(w)
    both = jnp.concatenate([hi.astype(BF16), lo.astype(BF16)], axis=1)
    d = lax.dot_general(left_rows(x), both, NT, preferred_element_type=F32)
    return d[:m] + d[m:]


def lane_gather(x, index):
    return jnp.take_along_axis(x, index, axis=1, mode="promise_in_bounds")


def order_kernel(panels, order, ordered, head, tail):
    leaves = order.shape[0]
    for i in range(leaves):
        at = slice(128 * i, 128 * (i + 1))
        index = jnp.broadcast_to(order[i : i + 1, :], (panels.shape[0], 128))
        placed = lane_gather(panels[:, at], index)
        ordered[:, at] = placed
        if i < W:
            head[:, at] = placed
        if i >= leaves - W:
            j = i - (leaves - W)
            tail[:, 128 * j : 128 * (j + 1)] = placed


def inverse_kernel(order, inverse):
    leaves = order.shape[0]
    rows = lax.broadcasted_iota(jnp.int32, (128, 128), 0)
    places = lax.broadcasted_iota(jnp.int32, (16, 128), 1).astype(F32).astype(BF16)
    for i in range(leaves):
        hot = (jnp.broadcast_to(order[i : i + 1, :], (128, 128)) == rows).astype(F32).astype(BF16)
        inv = lax.dot_general(places, hot, NT, preferred_element_type=F32)
        inverse[i : i + 1, :] = inv[0:1].astype(jnp.int32)


def up_kernel(ordered, basis, mats, pairs, packets):
    leaves = basis.shape[0]
    rank = basis.shape[1]
    count = leaves // 2
    nodes = []
    for j in range(count):
        x = ordered[:, 256 * j : 256 * (j + 1)]
        w = jnp.concatenate([basis[2 * j], basis[2 * j + 1]], axis=1)
        nodes.append(mul_nt(x, w) * ROOT_HALF)
    first_pair, first_node = 0, 0
    while count > 1:
        lifted = []
        for j in range(count // 2):
            pair = jnp.concatenate([nodes[2 * j], nodes[2 * j + 1]], axis=1)
            pairs[first_pair + j] = pair
            at = first_node + 2 * j
            w = mats[at : at + 2].reshape(2 * rank, 2 * rank)
            lifted.append(mul_nn(pair, w)[:, rank:] * ROOT_HALF)
        nodes = lifted
        first_pair += count // 2
        first_node += count
        count //= 2
    skel = nodes[0]
    lift = mul_nn(skel, mats[first_node])[:, rank:]
    packet = jnp.concatenate([skel, lift], axis=1)
    packets[...] = jnp.broadcast_to(packet[None], packets.shape)


def near_kernel(cols, own, arr1, arr2, arr3, rim0, rim1, rim2, rim3, tiles, out0, out1, out2, out3, held):
    leaves = tiles.shape[0]
    slots = tiles.shape[1]
    base = lax.axis_index("leaf") * leaves - W
    mains = (own, arr1, arr2, arr3)
    rims = (rim0, rim1, rim2, rim3)
    outs = (out0, out1, out2, out3)

    def hold(place, refs, column):
        at = pl.ds(column, 128)
        x = jnp.concatenate([ref[:, at] for ref in refs], axis=0)
        hi, lo = halves(x)
        held[place] = jnp.concatenate([hi.astype(BF16), lo.astype(BF16)], axis=0)

    for i in range(W):
        hold(i, rims, 128 * i)
        hold(i + W + leaves, rims, 128 * (i + W))

    def hold_main(i, carry):
        hold(i + W, mains, pl.multiple_of(i * 128, 128))
        return carry

    lax.fori_loop(0, leaves, hold_main, 0, unroll=8)

    def group(g, carry):
        parts = []
        for k in range(4):
            i = 4 * g + k
            x = jnp.concatenate([held[cols[i, n] - base] for n in range(slots)], axis=1)
            t = jnp.concatenate([tiles[i, n] for n in range(slots)], axis=1)
            hi, lo = halves(t)
            w = jnp.concatenate([hi.astype(BF16), lo.astype(BF16)], axis=0)
            d = lax.dot_general(x, w, NT, preferred_element_type=F32)
            m, q = d.shape[0] // 2, d.shape[1] // 2
            parts.append(d[:m, :q] + (d[:m, q:] + d[m:, :q]))
        rows = jnp.concatenate(parts, axis=1)
        at = pl.ds(pl.multiple_of(g * 128, 128), 128)
        for k in range(4):
            outs[k][:, at] = rows[8 * k : 8 * (k + 1)]
        return carry

    lax.fori_loop(0, leaves // 4, group, 0, unroll=2)


def down_kernel(cross_flags, flags, packets, pairs, basis, mats, coupling, transfer, far, skels):
    leaves = basis.shape[0]
    rank = basis.shape[1]
    devices = packets.shape[0]
    me = lax.axis_index("leaf")
    count = devices // 2
    nodes = [
        (packets[2 * j][:, rank:] + packets[2 * j + 1][:, rank:]) * ROOT_HALF for j in range(count)
    ]
    first = 0
    while count > 1:
        for j in range(count):
            skels[first + j] = nodes[j]
        if count > 2:
            lifted = []
            for j in range(count // 2):
                pair = jnp.concatenate([nodes[2 * j], nodes[2 * j + 1]], axis=1)
                at = first + 2 * j
                w = transfer[at : at + 2].reshape(2 * rank, rank)
                lifted.append(mul_nn(pair, w) * ROOT_HALF)
            nodes = lifted
        first += count
        count //= 2
    depth = devices.bit_length() - 1
    z = None
    for c in range(depth - 1, 0, -1):
        start = devices - (devices >> (c - 1))
        node = start + (me >> c)
        sibling = start + ((me >> c) ^ 1)
        x = skels[sibling] * cross_flags[node].astype(F32)
        w = coupling[node]
        if z is None:
            z = mul_nt(x, w)
        else:
            z = mul_nt(x, w) + mul_nt(z, transfer[node])
    top = leaves - 2
    x = jnp.concatenate([packets[me ^ 1][:, :rank] * flags[0, top].astype(F32), z], axis=1)
    zs = [mul_nt(x, mats[top])]
    count = 2
    while count < leaves:
        first_node = leaves - 2 * count
        first_pair = (leaves - 2 * count) // 2
        lower = []
        for j in range(count // 2):
            pair = pairs[first_pair + j]
            z = zs[j]
            for side in (0, 1):
                node = first_node + 2 * j + side
                other = pair[:, rank:] if side == 0 else pair[:, :rank]
                x = jnp.concatenate([other * flags[0, node].astype(F32), z], axis=1)
                lower.append(mul_nt(x, mats[node]))
        zs = lower
        count *= 2
    for j in range(leaves // 2):
        w = jnp.concatenate([basis[2 * j], basis[2 * j + 1]], axis=1)
        both = mul_nn(zs[j], w)
        far[:, 256 * j : 256 * (j + 1)] = both


def final_kernel(inverse, far, near0, near1, near2, near3, out):
    leaves = inverse.shape[0]
    me = lax.axis_index("vec")
    nears = (near0, near1, near2, near3)
    for i in range(leaves):
        index = jnp.broadcast_to(inverse[i : i + 1, :], (out.shape[0], 128))
        owner = ((index >> 5) - me) & 3
        place = (index & 31) + 32 * (i % 4)
        at = slice(128 * (i // 4), 128 * (i // 4 + 1))
        near = lane_gather(near0[:, at], place)
        for k in (1, 2, 3):
            near = jnp.where(owner == k, lane_gather(nears[k][:, at], place), near)
        spot = slice(128 * i, 128 * (i + 1))
        out[:, spot] = near + lane_gather(far[:, spot], index)


def call(kernel, ins, out_shapes, scratch=(), scalars=0):
    return pl.pallas_call(
        kernel,
        out_shape=[jax.ShapeDtypeStruct(s, t) for s, t in out_shapes],
        in_specs=[smem()] * scalars + [vmem()] * (len(ins) - scalars),
        out_specs=[vmem()] * len(out_shapes),
        scratch_shapes=list(scratch),
        compiler_params=params(),
    )(*ins)


def local(
    panels,
    near_tiles,
    near_cols,
    leaf_order,
    leaf_basis,
    local_mats,
    local_flags,
    cross_coupling,
    cross_transfer,
    cross_flags,
):
    rhs = panels.shape[0]
    leaves, rank, size = leaf_basis.shape
    devices = lax.axis_size("leaf")
    parts = lax.axis_size("vec")
    mats = local_mats[0]
    rim = W * size

    def turned(x, k):
        return lax.ppermute(x, "vec", [(i, (i + k) % parts) for i in range(parts)])

    ordered, head, tail = call(
        order_kernel,
        (panels, leaf_order),
        [((rhs, leaves * size), F32), ((rhs, rim), F32), ((rhs, rim), F32)],
    )
    ends = devices - 1
    before = lax.ppermute(tail, "leaf", [(i, i + 1) for i in range(ends)])
    after = lax.ppermute(head, "leaf", [(i + 1, i) for i in range(ends)])
    others = [turned(ordered, k) for k in (1, 2, 3)]
    rims = jnp.concatenate([before, after], axis=1)
    other_rims = [turned(rims, k) for k in (1, 2, 3)]

    pairs, packets = call(
        up_kernel,
        (ordered, leaf_basis, mats),
        [((leaves // 2 - 1, rhs, 2 * rank), F32), ((devices, rhs, 2 * rank), F32)],
    )
    gathered = lax.all_to_all(packets, "leaf", 0, 0)
    (inverse,) = call(inverse_kernel, (leaf_order,), [((leaves, size), jnp.int32)])

    near = call(
        near_kernel,
        (near_cols, ordered, *others, rims, *other_rims, near_tiles),
        [((rhs, leaves * near_tiles.shape[2]), F32)] * 4,
        scratch=[pltpu.VMEM((leaves + 2 * W, 2 * parts * rhs, size), BF16)],
        scalars=1,
    )
    back = [near[0]] + [turned(near[k], -k) for k in (1, 2, 3)]

    (far,) = call(
        down_kernel,
        (cross_flags, local_flags, gathered, pairs, leaf_basis, mats, cross_coupling, cross_transfer),
        [((rhs, leaves * size), F32)],
        scratch=[pltpu.VMEM((devices - 2, rhs, rank), F32)],
        scalars=2,
    )
    (out,) = call(final_kernel, (inverse, far, *back), [((rhs, leaves * size), F32)])
    return out


def solution(mesh):
    return jax.shard_map(
        local,
        mesh=mesh,
        in_specs=(
            P("vec", "leaf"),
            P("leaf", None, "vec", None),
            P("leaf", None),
            P("leaf", None),
            P("leaf", None, None),
            P("leaf", None, None, None),
            P("leaf", None),
            P(),
            P(),
            P(),
        ),
        out_specs=P("vec", "leaf"),
        check_vma=False,
    )
```

time: 149 us -> 71.8 us (0.48)
  matrix products: 50.3 us -> 0 us
  waiting for transfers between devices: 36.5 us -> 10.2 us
  Pallas kernels: 0 us -> 16.9 us
  between operations: 16.7 us -> 0.18 us
  starting transfers between devices: 27.5 us -> 29.7 us
  other arithmetic: 2.19 us -> 0 us
    dot_general x37 -> x0, matrix products: 50.3 us -> none  [the longest x5 9.07 us: local(): jnp.einsum('jkm,jsm->jsk', transfer, spread, precision=precise)]
    pallas_call x0 -> x6, Pallas kernels: none -> 16.9 us  [call(): pl.pallas_call(kernel, out_shape=[jax.ShapeDtypeStruct(s, t) for s, t in...]
    all_gather x1 -> x0, waiting for transfers between devices: 16.2 us -> none  [local(): extended = lax.all_gather(rimmed, 'vec', axis=0, tiled=True)]
    unnamed x17 -> x40, local copies, waits for them, and re-layouts: 4.23 us -> 13.8 us
    all_to_all x1, starting transfers between devices: 3.63 us -> 12 us  [local(): gathered = lax.all_to_all(packets, 'leaf', 0, 0)]
    ppermute x13 -> x11, waiting for transfers between devices: 16.7 us -> 10.2 us  [the longest x9 8.63 us: turned(): return lax.ppermute(x, 'vec', [(i, (i + k) % parts) for i in range(parts)])]
    slice x12 -> x0, local copies, waits for them, and re-layouts: 6.22 us -> none  [the longest x5 5.26 us: local(): blocks = local_blocks[first_node:first_node + node_count]]
    ppermute x13 -> x11, starting transfers between devices: 23.9 us -> 17.7 us  [the longest x9 10.9 us: turned(): return lax.ppermute(x, 'vec', [(i, (i + k) % parts) for i in range(parts)])]
  transfers between devices with their start and end apart: 15 -> 12, of which waited for: 9 -> 4; matrix products, arithmetic and copies ran while one was open for 20% -> 0% of each run, Pallas kernels for 0% -> 18%
where the time goes in v1:
time: 71.8 us; the launch traced here: 70.9 us
  starting transfers between devices  29.7 us (41%)
  Pallas kernels  16.9 us (24%)
  local copies, waits for them, and re-layouts  13.8 us (19%)
  waiting for transfers between devices  10.2 us (14%)
    pallas_call x6, Pallas kernels, call(): pl.pallas_call(kernel, out_shape=[jax.ShapeDtypeStruct(s, t) for s, t in...  16.9 us
    unnamed x40, local copies, waits for them, and re-layouts  13.8 us
    all_to_all x1, starting transfers between devices, local(): gathered = lax.all_to_all(packets, 'leaf', 0, 0)  12 us
    ppermute x9, starting transfers between devices, turned(): return lax.ppermute(x, 'vec', [(i, (i + k) % parts) for i in range(parts)])  10.9 us
    ppermute x9, waiting for transfers between devices, turned(): return lax.ppermute(x, 'vec', [(i, (i + k) % parts) for i in range(parts)])  8.63 us
    ppermute x1, starting transfers between devices, local(): after = lax.ppermute(head, 'leaf', [(i + 1, i) for i in range(ends)])  4.76 us
    ppermute x1, starting transfers between devices, local(): before = lax.ppermute(tail, 'leaf', [(i, i + 1) for i in range(ends)])  2.06 us
    ppermute x1, waiting for transfers between devices, local(): after = lax.ppermute(head, 'leaf', [(i + 1, i) for i in range(ends)])  1.55 us
  transfers between devices with their start and end apart: 12, of which 4 were waited for; matrix products, arithmetic and copies ran while one was open for 0% of the time, Pallas kernels for 18%

profile of v1, /device:TPU:2, one launch (start us, length us, event | category | flops | bytes accessed | tf_op | source)
XLA Modules:
  0.0 70.9 jit_solution(15659270487223908250)
XLA Ops:
  0.0 0.0 copy-start.5
  0.0 0.9 %copy-done.5 = f32[8,8192]{1,0:T(8,128)S(1)} copy-done((f32[8,8192]{1,0:T(8,128)S(1)}, f32[8,8192]{1,0:T(8,128)}, u32[]{:S(2)}) %copy-start.5) | copy-done | bytes 262168
  1.0 0.0 copy-start.6
  1.0 0.8 %copy-done.6 = s32[64,128]{1,0:T(8,128)S(1)} copy-done((s32[64,128]{1,0:T(8,128)S(1)}, s32[64,128]{1,0:T(8,128)}, u32[]{:S(2)}) %copy-start.6) | copy-done | bytes 32792
  1.7 0.2 shard_map.101
  1.9 0.0 copy-start
  1.9 1.6 %copy-done = f32[64,64,128]{2,1,0:T(8,128)S(1)} copy-done((f32[64,64,128]{2,1,0:T(8,128)S(1)}, f32[64,64,128]{2,1,0:T(8,128)}, u32[]{:S(2)}) %copy-start) | copy-done | bytes 2097176
  3.5 0.0 copy-start.1
  3.5 1.6 %copy-done.1 = f32[1,63,64,128]{3,2,1,0:T(8,128)S(1)} copy-done((f32[1,63,64,128]{3,2,1,0:T(8,128)S(1)}, f32[1,63,64,128]{3,2,1,0:T(8,128)}, u32[]{:S(2)}) %copy-start.1) | copy-done | bytes 2064408
  5.1 0.0 copy-start.18
  5.1 2.4 %shard_map.102 = (f32[31,8,128]{2,1,0:T(8,128)S(1)}, f32[64,8,128]{2,1,0:T(8,128)}) custom-call(f32[8,8192]{1,0:T(8,128)S(1)} %get-tuple-element.14.ordered.own, f32[64,64,128]{2,1,0:T(8,128)S(1)} %copy-done, f32[63,64,128]{2,1,0:T(8,128)S(1)} %bitcast.2), custom_call_target="tpu_custom_call" | custom-call | tf_op jit(solution)/shard_map/pallas_call | solution.py:232
  7.5 0.0 copy-start.8
  7.5 0.6 copy-done.8
  8.1 12.0 %all-to-all-start = ((f32[64,8,128]{2,1,0:T(8,128)}), f32[64,8,128]{2,1,0:T(8,128)S(1)}, u32[]{:S(2)}, u32[]{:S(2)}) async-start(f32[64,8,128]{2,1,0:T(8,128)} %get-tuple-element.15), calls=%async_computation | async-start | bytes 524288 | tf_op jit(solution)/shard_map/all_to_all | solution.py:281
  20.2 2.1 %collective-permute-start.3 = (f32[8,1024]{1,0:T(8,128)S(1)}, f32[8,1024]{1,0:T(8,128)S(1)}, u32[]{:S(2)}, u32[]{:S(2)}) collective-permute-start(f32[8,1024]{1,0:T(8,128)S(1)} %get-tuple-element.17), channel_id=1, source_target_pairs={{0,4},{4,8},{8,12},{12,16},{16,20},{20,24},{24,28},{28,32},{32,36}... | collective-permute-start | bytes 98312 | tf_op jit(solution)/shard_map/ppermute | solution.py:270
  22.2 1.7 %collective-permute-start = (f32[8,8192]{1,0:T(8,128)S(1)}, f32[8,8192]{1,0:T(8,128)S(1)}, u32[]{:S(2)}, u32[]{:S(2)}) collective-permute-start(f32[8,8192]{1,0:T(8,128)S(1)} %get-tuple-element.14.ordered.own), channel_id=1, source_target_pairs={{0,1},{1,2},{2,3},{3,0},{4,5},{5,6},{6,7},{7,4},{8,9},{9,10},{10,1... | collective-permute-start | bytes 786440 | tf_op jit(solution)/shard_map/ppermute | solution.py:262
  23.9 2.9 %collective-permute-start.1 = (f32[8,8192]{1,0:T(8,128)S(1)}, f32[8,8192]{1,0:T(8,128)S(1)}, u32[]{:S(2)}, u32[]{:S(2)}) collective-permute-start(f32[8,8192]{1,0:T(8,128)S(1)} %get-tuple-element.14.ordered.own), channel_id=1, source_target_pairs={{0,2},{1,3},{2,0},{3,1},{4,6},{5,7},{6,4},{7,5},{8,10},{9,11},{10,... | collective-permute-start | bytes 786440 | tf_op jit(solution)/shard_map/ppermute | solution.py:262
  26.8 1.3 %collective-permute-start.2 = (f32[8,8192]{1,0:T(8,128)S(1)}, f32[8,8192]{1,0:T(8,128)S(1)}, u32[]{:S(2)}, u32[]{:S(2)}) collective-permute-start(f32[8,8192]{1,0:T(8,128)S(1)} %get-tuple-element.14.ordered.own), channel_id=1, source_target_pairs={{0,3},{1,0},{2,1},{3,2},{4,7},{5,4},{6,5},{7,6},{8,11},{9,8},{10,9... | collective-permute-start | bytes 786440 | tf_op jit(solution)/shard_map/ppermute | solution.py:262
  28.1 4.8 %collective-permute-start.4 = (f32[8,1024]{1,0:T(8,128)S(1)}, f32[8,1024]{1,0:T(8,128)S(1)}, u32[]{:S(2)}, u32[]{:S(2)}) collective-permute-start(f32[8,1024]{1,0:T(8,128)S(1)} %get-tuple-element.18), channel_id=1, source_target_pairs={{4,0},{8,4},{12,8},{16,12},{20,16},{24,20},{28,24},{32,28},{36,32}... | collective-permute-start | bytes 98312 | tf_op jit(solution)/shard_map/ppermute | solution.py:271
  32.9 0.0 collective-permute-done.3
  32.9 1.6 %collective-permute-done.4 = f32[8,1024]{1,0:T(8,128)S(1)} collective-permute-done((f32[8,1024]{1,0:T(8,128)S(1)}, f32[8,1024]{1,0:T(8,128)S(1)}, u32[]{:S(2)}, u32[]{:S(2)}) %collective-permute-start.4) | collective-permute-done | bytes 32800 | tf_op jit(solution)/shard_map/ppermute | solution.py:271
  34.5 0.7 collective-permute-start.5
  35.2 1.1 %collective-permute-start.6 = (f32[8,2048]{1,0:T(8,128)S(1)}, f32[8,2048]{1,0:T(8,128)S(1)}, u32[]{:S(2)}, u32[]{:S(2)}) collective-permute-start(f32[8,2048]{1,0:T(8,128)S(1)} %constant_dynamic-update-slice_fusion.rim0), channel_id=1, source_target_pairs={{0,2},{1,3},{2,0},{3,1},{4,6},{5,7},{6,4},{7,5},{8,10},{9,11},{10,... | collective-permute-start | bytes 196616 | tf_op jit(solution)/shard_map/ppermute | solution.py:262
  36.2 5.1 %collective-permute-done.5.rim1 = f32[8,2048]{1,0:T(8,128)S(1)} collective-permute-done((f32[8,2048]{1,0:T(8,128)S(1)}, f32[8,2048]{1,0:T(8,128)S(1)}, u32[]{:S(2)}, u32[]{:S(2)}) %collective-permute-start.5) | collective-permute-done | bytes 65568 | tf_op jit(solution)/shard_map/ppermute | solution.py:262
  41.3 0.0 collective-permute-start.7
  41.3 0.0 copy-done.18
  41.3 0.0 copy-start.16
  41.4 0.0 copy-start.17
  41.4 0.1 copy.11.cols
  41.5 0.5 collective-permute-done.6.rim2
  42.0 0.0 copy-start.10
  42.0 0.6 copy-done.10
  42.6 3.0 %collective-permute-done.7.rim3 = f32[8,2048]{1,0:T(8,128)S(1)} collective-permute-done((f32[8,2048]{1,0:T(8,128)S(1)}, f32[8,2048]{1,0:T(8,128)S(1)}, u32[]{:S(2)}, u32[]{:S(2)}) %collective-permute-start.7) | collective-permute-done | bytes 65568 | tf_op jit(solution)/shard_map/ppermute | solution.py:262
  45.6 0.0 copy-start.12
  45.6 0.6 copy-done.12
  46.2 0.0 collective-permute-done.arr1
  46.2 0.0 collective-permute-done.1.arr2
  46.2 0.0 collective-permute-done.2.arr3
  46.2 0.0 copy-start.2
  46.2 2.2 %copy-done.2 = f32[64,4,32,128]{3,2,1,0:T(8,128)S(1)} copy-done((f32[64,4,32,128]{3,2,1,0:T(8,128)S(1)}, f32[64,4,32,128]{3,2,1,0:T(8,128)}, u32[]{:S(2)}) %copy-start.2) | copy-done | bytes 4194328
  48.4 0.0 copy-start.11
  48.4 0.8 %copy-done.11 = f32[8,2048]{1,0:T(8,128)S(1)} copy-done((f32[8,2048]{1,0:T(8,128)S(1)}, f32[8,2048]{1,0:T(8,128)}, u32[]{:S(2)}) %copy-start.11) | copy-done | bytes 65560
  49.3 0.0 copy-start.13
  49.3 0.8 %copy-done.13 = f32[8,2048]{1,0:T(8,128)S(1)} copy-done((f32[8,2048]{1,0:T(8,128)S(1)}, f32[8,2048]{1,0:T(8,128)}, u32[]{:S(2)}) %copy-start.13) | copy-done | bytes 65560
  50.1 6.0 %shard_map.104 = (f32[8,2048]{1,0:T(8,128)S(1)}, f32[8,2048]{1,0:T(8,128)}, f32[8,2048]{1,0:T(8,128)}, f32[8,2048]{1,0:T(8,128)}) custom-call(s32[64,4]{1,0:T(8,128)S(1)} %copy.11.cols, f32[8,8192]{1,0:T(8,128)S(1)} %get-tuple-element.14.ordered.own, f32[8,8192]{1,0:T(8,128)S(1)} %collective-permute-done.arr1, f32[8,8192]{1,0:T(8,128)S(1)} %collective-permute-done.1.arr2, ...), custom_call_target="tpu_custom_call" | custom-call | tf_op jit(solution)/shard_map/pallas_call | solution.py:232
  56.1 0.6 copy-done.14
  56.7 0.0 collective-permute-start.10
  56.7 3.2 %collective-permute-start.8 = (f32[8,2048]{1,0:T(8,128)}, f32[8,2048]{1,0:T(8,128)S(1)}, u32[]{:S(2)}, u32[]{:S(2)}) collective-permute-start(f32[8,2048]{1,0:T(8,128)} %get-tuple-element.20), channel_id=1, source_target_pairs={{0,3},{1,0},{2,1},{3,2},{4,7},{5,4},{6,5},{7,6},{8,11},{9,8},{10,9... | collective-permute-start | bytes 196616 | tf_op jit(solution)/shard_map/ppermute | solution.py:262
  59.9 0.0 collective-permute-start.9
  59.9 0.0 copy-done.7
  59.9 1.2 %shard_map.100.inverse = s32[64,128]{1,0:T(8,128)S(1)} custom-call(s32[64,128]{1,0:T(8,128)S(1)} %copy-done.7), custom_call_target="tpu_custom_call" | custom-call | tf_op jit(solution)/shard_map/pallas_call | solution.py:232
  61.1 0.0 all-to-all-done.packets
  61.1 0.0 copy-done.16
  61.2 0.0 copy-done.17
  61.2 0.0 copy-done.3
  61.2 0.0 copy-start.4
  61.2 1.5 %copy-done.4 = f32[60,64,64]{2,1,0:T(8,128)S(1)} copy-done((f32[60,64,64]{2,1,0:T(8,128)S(1)}, f32[60,64,64]{2,1,0:T(8,128)}, u32[]{:S(2)}) %copy-start.4) | copy-done | bytes 983064
  62.7 0.9 %copy-done.9 = f32[31,8,128]{2,1,0:T(8,128)S(1)} copy-done((f32[31,8,128]{2,1,0:T(8,128)S(1)}, f32[31,8,128]{2,1,0:T(8,128)}, u32[]{:S(2)}) %copy-start.9) | copy-done | bytes 127000
  63.6 5.7 %shard_map.103.far = f32[8,8192]{1,0:T(8,128)S(1)} custom-call(s32[62]{0:T(128)S(1)} %copy-done.16, s32[1,63]{1,0:T(1,128)S(1)} %copy-done.17, f32[64,8,128]{2,1,0:T(8,128)S(1)} %all-to-all-done.packets, f32[31,8,128]{2,1,0:T(8,128)S(1)} %copy-done.9, f32[64,64,128]{2,1,0:T(8,128)} %basis.3, f32[63,64,128]{2,1,0:T(8,128)} %bitcast.1, ...), custom_call_target="tpu_custom_call" | custom-call | tf_op jit(solution)/shard_map/pallas_call | solution.py:232
  69.4 0.0 collective-permute-done.10.near3
  69.4 0.0 collective-permute-done.8.near1
  69.4 0.0 collective-permute-done.9.near2
  69.4 0.0 copy-done.15
  69.4 1.5 %shard_map.105 = f32[8,8192]{1,0:T(8,128)} custom-call(s32[64,128]{1,0:T(8,128)S(1)} %shard_map.100.inverse, f32[8,8192]{1,0:T(8,128)S(1)} %shard_map.103.far, f32[8,2048]{1,0:T(8,128)S(1)} %copy-done.15, f32[8,2048]{1,0:T(8,128)S(1)} %collective-permute-done.8.near1, f32[8,2048]{1,0:T(8,128)S(1)} %collective-permute-done.9.near2, ...), custom_call_target="tpu_custom_call" | custom-call | tf_op jit(solution)/shard_map/pallas_call | solution.py:232
  (7 shorter events, 0.0 us)
Async XLA Ops:
  0.0 0.9 %copy-start.5 = (f32[8,8192]{1,0:T(8,128)S(1)}, f32[8,8192]{1,0:T(8,128)}, u32[]{:S(2)}) copy-start(f32[8,8192]{1,0:T(8,128)} %panels.1) | copy-start | bytes 786436
  1.0 0.8 %copy-start.6 = (s32[64,128]{1,0:T(8,128)S(1)}, s32[64,128]{1,0:T(8,128)}, u32[]{:S(2)}) copy-start(s32[64,128]{1,0:T(8,128)} %order.3) | copy-start | bytes 98308
  1.9 1.6 %copy-start = (f32[64,64,128]{2,1,0:T(8,128)S(1)}, f32[64,64,128]{2,1,0:T(8,128)}, u32[]{:S(2)}) copy-start(f32[64,64,128]{2,1,0:T(8,128)} %basis.3) | copy-start | bytes 6291460
  3.5 1.6 %copy-start.1 = (f32[1,63,64,128]{3,2,1,0:T(8,128)S(1)}, f32[1,63,64,128]{3,2,1,0:T(8,128)}, u32[]{:S(2)}) copy-start(f32[1,63,64,128]{3,2,1,0:T(8,128)} %param.15) | copy-start | bytes 6193156
  5.1 36.2 %copy-start.18 = (s32[64,4]{0,1:T(4,128)S(1)}, s32[64,4]{0,1:T(4,128)}, u32[]{:S(2)}) copy-start(s32[64,4]{0,1:T(4,128)} %param.12) | copy-start | bytes 3076
  7.5 0.6 copy-start.8
  8.1 53.0 %all-to-all-start = ((f32[64,8,128]{2,1,0:T(8,128)}), f32[64,8,128]{2,1,0:T(8,128)S(1)}, u32[]{:S(2)}, u32[]{:S(2)}) async-start(f32[64,8,128]{2,1,0:T(8,128)} %get-tuple-element.15), calls=%async_computation | async-start | bytes 524288 | tf_op jit(solution)/shard_map/all_to_all | solution.py:281
  20.2 12.7 %collective-permute-start.3 = (f32[8,1024]{1,0:T(8,128)S(1)}, f32[8,1024]{1,0:T(8,128)S(1)}, u32[]{:S(2)}, u32[]{:S(2)}) collective-permute-start(f32[8,1024]{1,0:T(8,128)S(1)} %get-tuple-element.17), channel_id=1, source_target_pairs={{0,4},{4,8},{8,12},{12,16},{16,20},{20,24},{24,28},{28,32},{32,36}... | collective-permute-start | bytes 98312 | tf_op jit(solution)/shard_map/ppermute | solution.py:270
  22.2 24.0 %collective-permute-start = (f32[8,8192]{1,0:T(8,128)S(1)}, f32[8,8192]{1,0:T(8,128)S(1)}, u32[]{:S(2)}, u32[]{:S(2)}) collective-permute-start(f32[8,8192]{1,0:T(8,128)S(1)} %get-tuple-element.14.ordered.own), channel_id=1, source_target_pairs={{0,1},{1,2},{2,3},{3,0},{4,5},{5,6},{6,7},{7,4},{8,9},{9,10},{10,1... | collective-permute-start | bytes 786440 | tf_op jit(solution)/shard_map/ppermute | solution.py:262
  23.9 22.3 %collective-permute-start.1 = (f32[8,8192]{1,0:T(8,128)S(1)}, f32[8,8192]{1,0:T(8,128)S(1)}, u32[]{:S(2)}, u32[]{:S(2)}) collective-permute-start(f32[8,8192]{1,0:T(8,128)S(1)} %get-tuple-element.14.ordered.own), channel_id=1, source_target_pairs={{0,2},{1,3},{2,0},{3,1},{4,6},{5,7},{6,4},{7,5},{8,10},{9,11},{10,... | collective-permute-start | bytes 786440 | tf_op jit(solution)/shard_map/ppermute | solution.py:262
  26.8 19.4 %collective-permute-start.2 = (f32[8,8192]{1,0:T(8,128)S(1)}, f32[8,8192]{1,0:T(8,128)S(1)}, u32[]{:S(2)}, u32[]{:S(2)}) collective-permute-start(f32[8,8192]{1,0:T(8,128)S(1)} %get-tuple-element.14.ordered.own), channel_id=1, source_target_pairs={{0,3},{1,0},{2,1},{3,2},{4,7},{5,4},{6,5},{7,6},{8,11},{9,8},{10,9... | collective-permute-start | bytes 786440 | tf_op jit(solution)/shard_map/ppermute | solution.py:262
  28.1 6.3 %collective-permute-start.4 = (f32[8,1024]{1,0:T(8,128)S(1)}, f32[8,1024]{1,0:T(8,128)S(1)}, u32[]{:S(2)}, u32[]{:S(2)}) collective-permute-start(f32[8,1024]{1,0:T(8,128)S(1)} %get-tuple-element.18), channel_id=1, source_target_pairs={{4,0},{8,4},{12,8},{16,12},{20,16},{24,20},{28,24},{32,28},{36,32}... | collective-permute-start | bytes 98312 | tf_op jit(solution)/shard_map/ppermute | solution.py:271
  34.5 6.9 %collective-permute-start.5 = (f32[8,2048]{1,0:T(8,128)S(1)}, f32[8,2048]{1,0:T(8,128)S(1)}, u32[]{:S(2)}, u32[]{:S(2)}) collective-permute-start(f32[8,2048]{1,0:T(8,128)S(1)} %constant_dynamic-update-slice_fusion.rim0), channel_id=1, source_target_pairs={{0,1},{1,2},{2,3},{3,0},{4,5},{5,6},{6,7},{7,4},{8,9},{9,10},{10,1... | collective-permute-start | bytes 196616 | tf_op jit(solution)/shard_map/ppermute | solution.py:262
  35.2 6.8 %collective-permute-start.6 = (f32[8,2048]{1,0:T(8,128)S(1)}, f32[8,2048]{1,0:T(8,128)S(1)}, u32[]{:S(2)}, u32[]{:S(2)}) collective-permute-start(f32[8,2048]{1,0:T(8,128)S(1)} %constant_dynamic-update-slice_fusion.rim0), channel_id=1, source_target_pairs={{0,2},{1,3},{2,0},{3,1},{4,6},{5,7},{6,4},{7,5},{8,10},{9,11},{10,... | collective-permute-start | bytes 196616 | tf_op jit(solution)/shard_map/ppermute | solution.py:262
  41.3 4.3 %collective-permute-start.7 = (f32[8,2048]{1,0:T(8,128)S(1)}, f32[8,2048]{1,0:T(8,128)S(1)}, u32[]{:S(2)}, u32[]{:S(2)}) collective-permute-start(f32[8,2048]{1,0:T(8,128)S(1)} %constant_dynamic-update-slice_fusion.rim0), channel_id=1, source_target_pairs={{0,3},{1,0},{2,1},{3,2},{4,7},{5,4},{6,5},{7,6},{8,11},{9,8},{10,9... | collective-permute-start | bytes 196616 | tf_op jit(solution)/shard_map/ppermute | solution.py:262
  41.3 18.6 %copy-start.7 = (s32[64,128]{1,0:T(8,128)S(1)}, s32[64,128]{1,0:T(8,128)}, u32[]{:S(2)}) copy-start(s32[64,128]{1,0:T(8,128)} %order.3) | copy-start | bytes 98308
  41.3 19.8 %copy-start.16 = (s32[62]{0:T(128)S(1)}, s32[62]{0:T(128)}, u32[]{:S(2)}) copy-start(s32[62]{0:T(128)} %cross_flags.1) | copy-start | bytes 748
  41.4 19.8 %copy-start.17 = (s32[1,63]{1,0:T(1,128)S(1)}, s32[1,63]{1,0:T(1,128)}, u32[]{:S(2)}) copy-start(s32[1,63]{1,0:T(1,128)} %flags.1) | copy-start | bytes 760
  42.0 0.6 copy-start.10
  45.6 0.6 copy-start.12
  46.2 2.2 %copy-start.2 = (f32[64,4,32,128]{3,2,1,0:T(8,128)S(1)}, f32[64,4,32,128]{3,2,1,0:T(8,128)}, u32[]{:S(2)}) copy-start(f32[64,4,32,128]{3,2,1,0:T(8,128)} %tiles.1) | copy-start | bytes 12582916
  48.4 0.8 %copy-start.11 = (f32[8,2048]{1,0:T(8,128)S(1)}, f32[8,2048]{1,0:T(8,128)}, u32[]{:S(2)}) copy-start(f32[8,2048]{1,0:T(8,128)} %copy-done.10) | copy-start | bytes 196612
  49.3 0.8 %copy-start.13 = (f32[8,2048]{1,0:T(8,128)S(1)}, f32[8,2048]{1,0:T(8,128)}, u32[]{:S(2)}) copy-start(f32[8,2048]{1,0:T(8,128)} %copy-done.12) | copy-start | bytes 196612
  50.1 11.1 %copy-start.3 = (f32[62,64,64]{2,1,0:T(8,128)S(1)}, f32[62,64,64]{2,1,0:T(8,128)}, u32[]{:S(2)}) copy-start(f32[62,64,64]{2,1,0:T(8,128)} %coupling.1) | copy-start | bytes 3047428
  56.1 0.6 copy-start.14
  56.7 12.7 %collective-permute-start.10 = (f32[8,2048]{1,0:T(8,128)}, f32[8,2048]{1,0:T(8,128)S(1)}, u32[]{:S(2)}, u32[]{:S(2)}) collective-permute-start(f32[8,2048]{1,0:T(8,128)} %get-tuple-element.22), channel_id=1, source_target_pairs={{0,1},{1,2},{2,3},{3,0},{4,5},{5,6},{6,7},{7,4},{8,9},{9,10},{10,1... | collective-permute-start | bytes 196616 | tf_op jit(solution)/shard_map/ppermute | solution.py:262
  56.7 12.7 %collective-permute-start.8 = (f32[8,2048]{1,0:T(8,128)}, f32[8,2048]{1,0:T(8,128)S(1)}, u32[]{:S(2)}, u32[]{:S(2)}) collective-permute-start(f32[8,2048]{1,0:T(8,128)} %get-tuple-element.20), channel_id=1, source_target_pairs={{0,3},{1,0},{2,1},{3,2},{4,7},{5,4},{6,5},{7,6},{8,11},{9,8},{10,9... | collective-permute-start | bytes 196616 | tf_op jit(solution)/shard_map/ppermute | solution.py:262
  59.9 9.5 %collective-permute-start.9 = (f32[8,2048]{1,0:T(8,128)}, f32[8,2048]{1,0:T(8,128)S(1)}, u32[]{:S(2)}, u32[]{:S(2)}) collective-permute-start(f32[8,2048]{1,0:T(8,128)} %get-tuple-element.21), channel_id=1, source_target_pairs={{0,2},{1,3},{2,0},{3,1},{4,6},{5,7},{6,4},{7,5},{8,10},{9,11},{10,... | collective-permute-start | bytes 196616 | tf_op jit(solution)/shard_map/ppermute | solution.py:262
  61.2 1.5 %copy-start.4 = (f32[60,64,64]{2,1,0:T(8,128)S(1)}, f32[60,64,64]{2,1,0:T(8,128)}, u32[]{:S(2)}) copy-start(f32[60,64,64]{2,1,0:T(8,128)} %transfer.1) | copy-start | bytes 2949124
  62.7 0.9 %copy-start.9 = (f32[31,8,128]{2,1,0:T(8,128)S(1)}, f32[31,8,128]{2,1,0:T(8,128)}, u32[]{:S(2)}) copy-start(f32[31,8,128]{2,1,0:T(8,128)} %copy-done.8) | copy-start | bytes 380932
  63.6 5.8 %copy-start.15 = (f32[8,2048]{1,0:T(8,128)S(1)}, f32[8,2048]{1,0:T(8,128)}, u32[]{:S(2)}) copy-start(f32[8,2048]{1,0:T(8,128)} %copy-done.14) | copy-start | bytes 196612

commit v2 on v1

--- a/solution.py
+++ b/solution.py
@@ -8,14 +8,18 @@
 from jax.sharding import PartitionSpec as P
 
 W = 8
+NEAR_US = 5
+EARLY = 1
+MIB = 52
+MIB0 = 52
 ROOT_HALF = 1.0 / math.sqrt(2.0)
 F32, BF16 = jnp.float32, jnp.bfloat16
 NN = (((1,), (0,)), ((), ()))
 NT = (((1,), (1,)), ((), ()))
 
 
-def params():
-    return pltpu.CompilerParams(vmem_limit_bytes=48 * 1024 * 1024)
+def params(mib):
+    return pltpu.CompilerParams(vmem_limit_bytes=int(mib * 1024 * 1024))
 
 
 def vmem():
@@ -24,6 +28,10 @@
 
 def smem():
     return pl.BlockSpec(memory_space=pltpu.SMEM)
+
+
+def hbm():
+    return pl.BlockSpec(memory_space=pltpu.HBM)
 
 
 def halves(x):
@@ -57,18 +65,32 @@
     return jnp.take_along_axis(x, index, axis=1, mode="promise_in_bounds")
 
 
-def order_kernel(panels, order, ordered, head, tail):
+def order_kernel(panels_hbm, order_hbm, middle, head, tail, panels, order, sems):
+    copies = [
+        pltpu.make_async_copy(order_hbm, order, sems.at[0]),
+        pltpu.make_async_copy(panels_hbm, panels, sems.at[1]),
+    ]
+    for copy in copies:
+        copy.start()
+    for copy in copies:
+        copy.wait()
     leaves = order.shape[0]
     for i in range(leaves):
-        at = slice(128 * i, 128 * (i + 1))
         index = jnp.broadcast_to(order[i : i + 1, :], (panels.shape[0], 128))
-        placed = lane_gather(panels[:, at], index)
-        ordered[:, at] = placed
+        placed = lane_gather(panels[:, 128 * i : 128 * (i + 1)], index)
+        middle[:, 128 * (i + W) : 128 * (i + W + 1)] = placed
         if i < W:
-            head[:, at] = placed
+            head[:, 128 * i : 128 * (i + 1)] = placed
         if i >= leaves - W:
             j = i - (leaves - W)
             tail[:, 128 * j : 128 * (j + 1)] = placed
+
+
+def rim_kernel(middle, before, after, extended):
+    del middle
+    width = before.shape[1]
+    extended[:, :width] = before[...]
+    extended[:, extended.shape[1] - width :] = after[...]
 
 
 def inverse_kernel(order, inverse):
@@ -81,17 +103,25 @@
         inverse[i : i + 1, :] = inv[0:1].astype(jnp.int32)
 
 
-def up_kernel(ordered, basis, mats, pairs, packets):
+def up_kernel(middle, basis_hbm, mats_hbm, pairs, packets, basis, mats, basis_sems, mats_sems):
     leaves = basis.shape[0]
     rank = basis.shape[1]
     count = leaves // 2
     nodes = []
+    chunks = basis_sems.shape[0]
+    basis_copies = chunked(basis_hbm, basis, basis_sems, chunks)
+    mats_copies = chunked(mats_hbm, mats, mats_sems, 2)
     for j in range(count):
-        x = ordered[:, 256 * j : 256 * (j + 1)]
+        if j % (count // chunks) == 0:
+            basis_copies[j // (count // chunks)].wait()
+        x = middle[:, 128 * (2 * j + W) : 128 * (2 * j + 2 + W)]
         w = jnp.concatenate([basis[2 * j], basis[2 * j + 1]], axis=1)
         nodes.append(mul_nt(x, w) * ROOT_HALF)
     first_pair, first_node = 0, 0
+    mats_copies[0].wait()
     while count > 1:
+        if first_node == leaves // 2:
+            mats_copies[1].wait()
         lifted = []
         for j in range(count // 2):
             pair = jnp.concatenate([nodes[2 * j], nodes[2 * j + 1]], axis=1)
@@ -109,35 +139,27 @@
     packets[...] = jnp.broadcast_to(packet[None], packets.shape)
 
 
-def near_kernel(cols, own, arr1, arr2, arr3, rim0, rim1, rim2, rim3, tiles, out0, out1, out2, out3, held):
+def near_kernel(cols, own, arr1, arr2, arr3, tiles_hbm, out0, out1, out2, out3, held, tiles, sems):
+    copies = chunked(tiles_hbm, tiles, sems, 4)
     leaves = tiles.shape[0]
     slots = tiles.shape[1]
     base = lax.axis_index("leaf") * leaves - W
-    mains = (own, arr1, arr2, arr3)
-    rims = (rim0, rim1, rim2, rim3)
     outs = (out0, out1, out2, out3)
 
-    def hold(place, refs, column):
-        at = pl.ds(column, 128)
-        x = jnp.concatenate([ref[:, at] for ref in refs], axis=0)
+    def hold(i, carry):
+        at = pl.ds(pl.multiple_of(i * 128, 128), 128)
+        x = jnp.concatenate([ref[:, at] for ref in (own, arr1, arr2, arr3)], axis=0)
         hi, lo = halves(x)
-        held[place] = jnp.concatenate([hi.astype(BF16), lo.astype(BF16)], axis=0)
-
-    for i in range(W):
-        hold(i, rims, 128 * i)
-        hold(i + W + leaves, rims, 128 * (i + W))
-
-    def hold_main(i, carry):
-        hold(i + W, mains, pl.multiple_of(i * 128, 128))
+        held[i] = jnp.concatenate([hi.astype(BF16), lo.astype(BF16)], axis=0)
         return carry
 
-    lax.fori_loop(0, leaves, hold_main, 0, unroll=8)
+    lax.fori_loop(0, leaves + 2 * W, hold, 0, unroll=8)
 
     def group(g, carry):
         parts = []
         for k in range(4):
             i = 4 * g + k
-            x = jnp.concatenate([held[cols[i, n] - base] for n in range(slots)], axis=1)
+            x = jnp.concatenate([held[cols[n, i] - base] for n in range(slots)], axis=1)
             t = jnp.concatenate([tiles[i, n] for n in range(slots)], axis=1)
             hi, lo = halves(t)
             w = jnp.concatenate([hi.astype(BF16), lo.astype(BF16)], axis=0)
@@ -150,19 +172,40 @@
             outs[k][:, at] = rows[8 * k : 8 * (k + 1)]
         return carry
 
-    lax.fori_loop(0, leaves // 4, group, 0, unroll=2)
-
-
-def down_kernel(cross_flags, flags, packets, pairs, basis, mats, coupling, transfer, far, skels):
+    quarter = leaves // 16
+    for c in range(4):
+        copies[c].wait()
+        lax.fori_loop(c * quarter, (c + 1) * quarter, group, 0, unroll=2)
+
+
+def down_kernel(
+    cross_flags, flags, packets, pairs, basis_hbm, mats_hbm, coupling_hbm, transfer_hbm,
+    far, skels, basis, mats, coupling, transfer, sems,
+):
     leaves = basis.shape[0]
     rank = basis.shape[1]
     devices = packets.shape[0]
+    depth = devices.bit_length() - 1
     me = lax.axis_index("leaf")
+    transfer_copy = pltpu.make_async_copy(transfer_hbm, transfer, sems.at[0])
+    transfer_copy.start()
+    coupling_copies = []
+    for c in range(1, depth):
+        node = devices - (devices >> (c - 1)) + (me >> c)
+        coupling_copies.append(
+            pltpu.make_async_copy(coupling_hbm.at[node], coupling.at[c - 1], sems.at[2 + c])
+        )
+        coupling_copies[-1].start()
+    mats_copy = pltpu.make_async_copy(mats_hbm, mats, sems.at[1])
+    mats_copy.start()
+    basis_copy = pltpu.make_async_copy(basis_hbm, basis, sems.at[2])
+    basis_copy.start()
     count = devices // 2
     nodes = [
         (packets[2 * j][:, rank:] + packets[2 * j + 1][:, rank:]) * ROOT_HALF for j in range(count)
     ]
     first = 0
+    transfer_copy.wait()
     while count > 1:
         for j in range(count):
             skels[first + j] = nodes[j]
@@ -176,20 +219,22 @@
             nodes = lifted
         first += count
         count //= 2
-    depth = devices.bit_length() - 1
+    for copy in coupling_copies:
+        copy.wait()
     z = None
     for c in range(depth - 1, 0, -1):
         start = devices - (devices >> (c - 1))
         node = start + (me >> c)
         sibling = start + ((me >> c) ^ 1)
         x = skels[sibling] * cross_flags[node].astype(F32)
-        w = coupling[node]
+        w = coupling[c - 1]
         if z is None:
             z = mul_nt(x, w)
         else:
             z = mul_nt(x, w) + mul_nt(z, transfer[node])
     top = leaves - 2
     x = jnp.concatenate([packets[me ^ 1][:, :rank] * flags[0, top].astype(F32), z], axis=1)
+    mats_copy.wait()
     zs = [mul_nt(x, mats[top])]
     count = 2
     while count < leaves:
@@ -206,6 +251,7 @@
                 lower.append(mul_nt(x, mats[node]))
         zs = lower
         count *= 2
+    basis_copy.wait()
     for j in range(leaves // 2):
         w = jnp.concatenate([basis[2 * j], basis[2 * j + 1]], axis=1)
         both = mul_nn(zs[j], w)
@@ -228,15 +274,28 @@
         out[:, spot] = near + lane_gather(far[:, spot], index)
 
 
-def call(kernel, ins, out_shapes, scratch=(), scalars=0):
+def call(kernel, spaces, ins, out_shapes, scratch=(), mib=0, us=0, alias={}):
+    place = {"s": smem, "v": vmem, "h": hbm}
     return pl.pallas_call(
         kernel,
         out_shape=[jax.ShapeDtypeStruct(s, t) for s, t in out_shapes],
-        in_specs=[smem()] * scalars + [vmem()] * (len(ins) - scalars),
+        in_specs=[place[k]() for k in spaces],
         out_specs=[vmem()] * len(out_shapes),
         scratch_shapes=list(scratch),
-        compiler_params=params(),
+        input_output_aliases=alias,
+        compiler_params=params(mib or MIB),
+        cost_estimate=pl.CostEstimate(flops=int(us * 1.15e9), bytes_accessed=0, transcendentals=0) if us else None,
     )(*ins)
+
+
+def chunked(source, target, sems, chunks):
+    step = -(-source.shape[0] // chunks)
+    copies = []
+    for c in range(chunks):
+        at = pl.ds(c * step, min(step, source.shape[0] - c * step))
+        copies.append(pltpu.make_async_copy(source.at[at], target.at[at], sems.at[c]))
+        copies[-1].start()
+    return copies
 
 
 def local(
@@ -261,43 +320,72 @@
     def turned(x, k):
         return lax.ppermute(x, "vec", [(i, (i + k) % parts) for i in range(parts)])
 
-    ordered, head, tail = call(
+    dma = pltpu.SemaphoreType.DMA
+
+    def up(source):
+        return call(
+            up_kernel,
+            "vhh",
+            (source, leaf_basis, mats),
+            [((leaves // 2 - 1, rhs, 2 * rank), F32), ((devices, rhs, 2 * rank), F32)],
+            [basis_shape, mats_shape, dma((8,)), dma((2,))],
+        )
+
+    basis_shape = pltpu.VMEM(leaf_basis.shape, F32)
+    mats_shape = pltpu.VMEM(mats.shape, F32)
+    length = (leaves + 2 * W) * size
+    middle, head, tail = call(
         order_kernel,
+        "hh",
         (panels, leaf_order),
-        [((rhs, leaves * size), F32), ((rhs, rim), F32), ((rhs, rim), F32)],
+        [((rhs, length), F32), ((rhs, rim), F32), ((rhs, rim), F32)],
+        [pltpu.VMEM(panels.shape, F32), pltpu.VMEM(leaf_order.shape, jnp.int32), dma((2,))],
+        MIB0,
     )
     ends = devices - 1
     before = lax.ppermute(tail, "leaf", [(i, i + 1) for i in range(ends)])
     after = lax.ppermute(head, "leaf", [(i + 1, i) for i in range(ends)])
-    others = [turned(ordered, k) for k in (1, 2, 3)]
-    rims = jnp.concatenate([before, after], axis=1)
-    other_rims = [turned(rims, k) for k in (1, 2, 3)]
-
-    pairs, packets = call(
-        up_kernel,
-        (ordered, leaf_basis, mats),
-        [((leaves // 2 - 1, rhs, 2 * rank), F32), ((devices, rhs, 2 * rank), F32)],
-    )
+    (inverse,) = call(inverse_kernel, "v", (leaf_order,), [((leaves, size), jnp.int32)])
+    if EARLY:
+        pairs, packets = up(middle)
+        middle, before, after, packets = lax.optimization_barrier((middle, before, after, packets))
+    if EARLY == 2:
+        middle, before, after, inverse = lax.optimization_barrier((middle, before, after, inverse))
+    (own,) = call(rim_kernel, "vvv", (middle, before, after), [((rhs, length), F32)], alias={0: 0})
+    others = [turned(own, k) for k in (1, 2, 3)]
+    if not EARLY:
+        pairs, packets = up(own)
     gathered = lax.all_to_all(packets, "leaf", 0, 0)
-    (inverse,) = call(inverse_kernel, (leaf_order,), [((leaves, size), jnp.int32)])
-
     near = call(
         near_kernel,
-        (near_cols, ordered, *others, rims, *other_rims, near_tiles),
+        "svvvvh",
+        (near_cols.T, own, *others, near_tiles),
         [((rhs, leaves * near_tiles.shape[2]), F32)] * 4,
-        scratch=[pltpu.VMEM((leaves + 2 * W, 2 * parts * rhs, size), BF16)],
-        scalars=1,
+        [
+            pltpu.VMEM((leaves + 2 * W, 2 * parts * rhs, size), BF16),
+            pltpu.VMEM(near_tiles.shape, F32),
+            dma((4,)),
+        ],
+        0,
+        NEAR_US,
     )
     back = [near[0]] + [turned(near[k], -k) for k in (1, 2, 3)]
 
     (far,) = call(
         down_kernel,
+        "ssvvhhhh",
         (cross_flags, local_flags, gathered, pairs, leaf_basis, mats, cross_coupling, cross_transfer),
         [((rhs, leaves * size), F32)],
-        scratch=[pltpu.VMEM((devices - 2, rhs, rank), F32)],
-        scalars=2,
+        [
+            pltpu.VMEM((devices - 2, rhs, rank), F32),
+            basis_shape,
+            mats_shape,
+            pltpu.VMEM((devices.bit_length() - 2, rank, rank), F32),
+            pltpu.VMEM(cross_transfer.shape, F32),
+            dma((devices.bit_length() + 2,)),
+        ],
     )
-    (out,) = call(final_kernel, (inverse, far, *back), [((rhs, leaves * size), F32)])
+    (out,) = call(final_kernel, "vvvvvv", (inverse, far, *back), [((rhs, leaves * size), F32)])
     return out
 
 

time: 71.8 us -> 52.1 us (0.73)
  the two profiles are of different devices: /device:TPU:2 before, /device:TPU:112 now
where the time goes in v2:
time: 52.1 us; the launch traced here: 51.9 us
  starting transfers between devices  26.5 us (51%)
  Pallas kernels  19.2 us (37%)
  waiting for transfers between devices  4.3 us (8%)
  local copies, waits for them, and re-layouts  1.73 us (3%)
    pallas_call x7, Pallas kernels, call(): pl.pallas_call(kernel, out_shape=[jax.ShapeDtypeStruct(s, t) for s, t in...  19.2 us
    all_to_all x1, starting transfers between devices, local(): gathered = lax.all_to_all(packets, 'leaf', 0, 0)  11.9 us
    ppermute x6, starting transfers between devices, turned(): return lax.ppermute(x, 'vec', [(i, (i + k) % parts) for i in range(parts)])  9.04 us
    ppermute x6, waiting for transfers between devices, turned(): return lax.ppermute(x, 'vec', [(i, (i + k) % parts) for i in range(parts)])  4.29 us
    ppermute x1, starting transfers between devices, local(): after = lax.ppermute(head, 'leaf', [(i + 1, i) for i in range(ends)])  3.64 us
    ppermute x1, starting transfers between devices, local(): before = lax.ppermute(tail, 'leaf', [(i, i + 1) for i in range(ends)])  1.92 us
    unnamed x12, local copies, waits for them, and re-layouts  1.73 us
  transfers between devices with their start and end apart: 9, of which 1 were waited for; matrix products, arithmetic and copies ran while one was open for 0% of the time, Pallas kernels for 34%

profile of v2, /device:TPU:112, one launch (start us, length us, event | category | flops | bytes accessed | tf_op | source)
XLA Modules:
  0.0 51.9 jit_solution(16649421685928020716)
XLA Ops:
  0.0 0.0 copy-start
  0.0 0.9 %copy-done = f32[8,8192]{1,0:T(8,128)S(1)} copy-done((f32[8,8192]{1,0:T(8,128)S(1)}, f32[8,8192]{1,0:T(8,128)}, u32[]{:S(2)}) %copy-start) | copy-done | bytes 262168
  1.0 0.0 copy-start.1
  1.0 0.8 %copy-done.1 = s32[64,128]{1,0:T(8,128)S(1)} copy-done((s32[64,128]{1,0:T(8,128)S(1)}, s32[64,128]{1,0:T(8,128)}, u32[]{:S(2)}) %copy-start.1) | copy-done | bytes 32792
  1.7 0.3 shard_map.101
  2.0 1.9 %collective-permute-start = (f32[8,1024]{1,0:T(8,128)S(1)}, f32[8,1024]{1,0:T(8,128)S(1)}, u32[]{:S(2)}, u32[]{:S(2)}) collective-permute-start(f32[8,1024]{1,0:T(8,128)S(1)} %get-tuple-element.19), channel_id=1, source_target_pairs={{0,4},{4,8},{8,12},{12,16},{16,20},{20,24},{24,28},{28,32},{32,36}... | collective-permute-start | bytes 98312 | tf_op jit(solution)/shard_map/ppermute | solution.py:346
  3.9 3.6 %collective-permute-start.1 = (f32[8,1024]{1,0:T(8,128)S(1)}, f32[8,1024]{1,0:T(8,128)S(1)}, u32[]{:S(2)}, u32[]{:S(2)}) collective-permute-start(f32[8,1024]{1,0:T(8,128)S(1)} %get-tuple-element.20), channel_id=1, source_target_pairs={{4,0},{8,4},{12,8},{16,12},{20,16},{24,20},{28,24},{32,28},{36,32}... | collective-permute-start | bytes 98312 | tf_op jit(solution)/shard_map/ppermute | solution.py:347
  7.6 0.0 copy-start.5
  7.6 4.5 %shard_map.102 = (f32[31,8,128]{2,1,0:T(8,128)S(1)}, f32[64,8,128]{2,1,0:T(8,128)}) custom-call(f32[8,10240]{1,0:T(8,128)S(1)} %get-tuple-element.24.middle, f32[64,64,128]{2,1,0:T(8,128)} %basis_hbm.3, f32[63,64,128]{2,1,0:T(8,128)} %bitcast.3), custom_call_target="tpu_custom_call" | custom-call | tf_op jit(solution)/shard_map/pallas_call | solution.py:279
  12.1 0.0 collective-permute-done.before
  12.1 0.0 collective-permute-done.1.after
  12.2 0.5 %collective-permute-start.4 = (f32[8,10240]{1,0:T(8,128)S(1)}, f32[8,10240]{1,0:T(8,128)S(1)}, u32[]{:S(2)}, u32[]{:S(2)}) collective-permute-start(f32[8,10240]{1,0:T(8,128)S(1)} %shard_map.104.own), channel_id=1, source_target_pairs={{0,3},{1,0},{2,1},{3,2},{4,7},{5,4},{6,5},{7,6},{8,11},{9,8},{10,9... | collective-permute-start | bytes 983048 | tf_op jit(solution)/shard_map/ppermute | solution.py:321
  12.7 2.9 %collective-permute-start.3 = (f32[8,10240]{1,0:T(8,128)S(1)}, f32[8,10240]{1,0:T(8,128)S(1)}, u32[]{:S(2)}, u32[]{:S(2)}) collective-permute-start(f32[8,10240]{1,0:T(8,128)S(1)} %shard_map.104.own), channel_id=1, source_target_pairs={{0,2},{1,3},{2,0},{3,1},{4,6},{5,7},{6,4},{7,5},{8,10},{9,11},{10,... | collective-permute-start | bytes 983048 | tf_op jit(solution)/shard_map/ppermute | solution.py:321
  15.6 0.0 collective-permute-start.2
  15.6 11.9 %all-to-all-start = ((f32[64,8,128]{2,1,0:T(8,128)}), f32[64,8,128]{2,1,0:T(8,128)S(1)}, u32[]{:S(2)}, u32[]{:S(2)}) async-start(f32[64,8,128]{2,1,0:T(8,128)} %get-tuple-element.22), calls=%async_computation | async-start | bytes 524288 | tf_op jit(solution)/shard_map/all_to_all | solution.py:358
  27.5 0.0 collective-permute-done.4.arr3
  27.5 0.0 collective-permute-done.3.arr2
  27.5 4.3 %collective-permute-done.2.arr1 = f32[8,10240]{1,0:T(8,128)S(1)} collective-permute-done((f32[8,10240]{1,0:T(8,128)S(1)}, f32[8,10240]{1,0:T(8,128)S(1)}, u32[]{:S(2)}, u32[]{:S(2)}) %collective-permute-start.2) | collective-permute-done | bytes 327712 | tf_op jit(solution)/shard_map/ppermute | solution.py:321
  31.8 0.0 copy-done.5
  31.8 0.0 copy-start.2
  31.8 0.0 copy-start.3
  31.8 0.0 copy-start.4
  31.8 5.8 %shard_map.105 = (f32[8,2048]{1,0:T(8,128)S(1)}, f32[8,2048]{1,0:T(8,128)S(1)}, f32[8,2048]{1,0:T(8,128)S(1)}, f32[8,2048]{1,0:T(8,128)S(1)}) custom-call(s32[4,64]{1,0:T(4,128)S(1)} %bitcast.2, f32[8,10240]{1,0:T(8,128)S(1)} %shard_map.104.own, f32[8,10240]{1,0:T(8,128)S(1)} %collective-permute-done.2.arr1, f32[8,10240]{1,0:T(8,128)S(1)} %collective-permute-done.3.arr2, ...), custom_call_target="tpu_custom_call" | custom-call | flops 5750000128 | tf_op jit(solution)/shard_map/pallas_call | solution.py:279
  37.7 0.4 collective-permute-start.5
  38.1 2.9 %collective-permute-start.6 = (f32[8,2048]{1,0:T(8,128)S(1)}, f32[8,2048]{1,0:T(8,128)S(1)}, u32[]{:S(2)}, u32[]{:S(2)}) collective-permute-start(f32[8,2048]{1,0:T(8,128)S(1)} %get-tuple-element.29), channel_id=1, source_target_pairs={{0,2},{1,3},{2,0},{3,1},{4,6},{5,7},{6,4},{7,5},{8,10},{9,11},{10,... | collective-permute-start | bytes 196616 | tf_op jit(solution)/shard_map/ppermute | solution.py:321
  40.9 2.3 %collective-permute-start.7 = (f32[8,2048]{1,0:T(8,128)S(1)}, f32[8,2048]{1,0:T(8,128)S(1)}, u32[]{:S(2)}, u32[]{:S(2)}) collective-permute-start(f32[8,2048]{1,0:T(8,128)S(1)} %get-tuple-element.30), channel_id=1, source_target_pairs={{0,1},{1,2},{2,3},{3,0},{4,5},{5,6},{6,7},{7,4},{8,9},{9,10},{10,1... | collective-permute-start | bytes 196616 | tf_op jit(solution)/shard_map/ppermute | solution.py:321
  43.3 0.0 copy-done.2
  43.3 1.2 %shard_map.100.inverse = s32[64,128]{1,0:T(8,128)S(1)} custom-call(s32[64,128]{1,0:T(8,128)S(1)} %copy-done.2), custom_call_target="tpu_custom_call" | custom-call | tf_op jit(solution)/shard_map/pallas_call | solution.py:279
  44.5 0.0 all-to-all-done.packets
  44.5 0.0 copy-done.3
  44.5 0.0 copy-done.4
  44.5 5.9 %shard_map.103.far = f32[8,8192]{1,0:T(8,128)S(1)} custom-call(s32[62]{0:T(128)S(1)} %copy-done.3, s32[1,63]{1,0:T(1,128)S(1)} %copy-done.4, f32[64,8,128]{2,1,0:T(8,128)S(1)} %all-to-all-done.packets, f32[31,8,128]{2,1,0:T(8,128)S(1)} %get-tuple-element.23.pairs, f32[64,64,128]{2,1,0:T(8,128)} %basis_hbm.3, f32[63,64,128]{2,1,0:T(8,128)} %bitcast.4, ...), custom_call_target="tpu_custom_call" | custom-call | tf_op jit(solution)/shard_map/pallas_call | solution.py:279
  50.4 0.0 collective-permute-done.5.near1
  50.4 0.0 collective-permute-done.6.near2
  50.4 0.0 collective-permute-done.7.near3
  50.4 1.5 %shard_map.106 = f32[8,8192]{1,0:T(8,128)} custom-call(s32[64,128]{1,0:T(8,128)S(1)} %shard_map.100.inverse, f32[8,8192]{1,0:T(8,128)S(1)} %shard_map.103.far, f32[8,2048]{1,0:T(8,128)S(1)} %get-tuple-element.27.near0, f32[8,2048]{1,0:T(8,128)S(1)} %collective-permute-done.5.near1, f32[8,2048]{1,0:T(8,128)S(1)} %collective-permute-done.6.near2, ...), custom_call_target="tpu_custom_call" | custom-call | tf_op jit(solution)/shard_map/pallas_call | solution.py:279
  (1 shorter events, 0.0 us)
Async XLA Ops:
  0.0 0.9 %copy-start = (f32[8,8192]{1,0:T(8,128)S(1)}, f32[8,8192]{1,0:T(8,128)}, u32[]{:S(2)}) copy-start(f32[8,8192]{1,0:T(8,128)} %panels_hbm.1) | copy-start | bytes 786436
  1.0 0.8 %copy-start.1 = (s32[64,128]{1,0:T(8,128)S(1)}, s32[64,128]{1,0:T(8,128)}, u32[]{:S(2)}) copy-start(s32[64,128]{1,0:T(8,128)} %order_hbm.1) | copy-start | bytes 98308
  2.0 10.1 %collective-permute-start = (f32[8,1024]{1,0:T(8,128)S(1)}, f32[8,1024]{1,0:T(8,128)S(1)}, u32[]{:S(2)}, u32[]{:S(2)}) collective-permute-start(f32[8,1024]{1,0:T(8,128)S(1)} %get-tuple-element.19), channel_id=1, source_target_pairs={{0,4},{4,8},{8,12},{12,16},{16,20},{20,24},{24,28},{28,32},{32,36}... | collective-permute-start | bytes 98312 | tf_op jit(solution)/shard_map/ppermute | solution.py:346
  3.9 8.2 %collective-permute-start.1 = (f32[8,1024]{1,0:T(8,128)S(1)}, f32[8,1024]{1,0:T(8,128)S(1)}, u32[]{:S(2)}, u32[]{:S(2)}) collective-permute-start(f32[8,1024]{1,0:T(8,128)S(1)} %get-tuple-element.20), channel_id=1, source_target_pairs={{4,0},{8,4},{12,8},{16,12},{20,16},{24,20},{28,24},{32,28},{36,32}... | collective-permute-start | bytes 98312 | tf_op jit(solution)/shard_map/ppermute | solution.py:347
  7.6 24.2 %copy-start.5 = (s32[64,4]{0,1:T(4,128)S(1)}, s32[64,4]{0,1:T(4,128)}, u32[]{:S(2)}) copy-start(s32[64,4]{0,1:T(4,128)} %param.12) | copy-start | bytes 3076
  12.2 15.3 %collective-permute-start.4 = (f32[8,10240]{1,0:T(8,128)S(1)}, f32[8,10240]{1,0:T(8,128)S(1)}, u32[]{:S(2)}, u32[]{:S(2)}) collective-permute-start(f32[8,10240]{1,0:T(8,128)S(1)} %shard_map.104.own), channel_id=1, source_target_pairs={{0,3},{1,0},{2,1},{3,2},{4,7},{5,4},{6,5},{7,6},{8,11},{9,8},{10,9... | collective-permute-start | bytes 983048 | tf_op jit(solution)/shard_map/ppermute | solution.py:321
  12.7 14.8 %collective-permute-start.3 = (f32[8,10240]{1,0:T(8,128)S(1)}, f32[8,10240]{1,0:T(8,128)S(1)}, u32[]{:S(2)}, u32[]{:S(2)}) collective-permute-start(f32[8,10240]{1,0:T(8,128)S(1)} %shard_map.104.own), channel_id=1, source_target_pairs={{0,2},{1,3},{2,0},{3,1},{4,6},{5,7},{6,4},{7,5},{8,10},{9,11},{10,... | collective-permute-start | bytes 983048 | tf_op jit(solution)/shard_map/ppermute | solution.py:321
  15.6 16.2 %collective-permute-start.2 = (f32[8,10240]{1,0:T(8,128)S(1)}, f32[8,10240]{1,0:T(8,128)S(1)}, u32[]{:S(2)}, u32[]{:S(2)}) collective-permute-start(f32[8,10240]{1,0:T(8,128)S(1)} %shard_map.104.own), channel_id=1, source_target_pairs={{0,1},{1,2},{2,3},{3,0},{4,5},{5,6},{6,7},{7,4},{8,9},{9,10},{10,1... | collective-permute-start | bytes 983048 | tf_op jit(solution)/shard_map/ppermute | solution.py:321
  15.6 28.9 %all-to-all-start = ((f32[64,8,128]{2,1,0:T(8,128)}), f32[64,8,128]{2,1,0:T(8,128)S(1)}, u32[]{:S(2)}, u32[]{:S(2)}) async-start(f32[64,8,128]{2,1,0:T(8,128)} %get-tuple-element.22), calls=%async_computation | async-start | bytes 524288 | tf_op jit(solution)/shard_map/all_to_all | solution.py:358
  31.8 11.5 %copy-start.2 = (s32[64,128]{1,0:T(8,128)S(1)}, s32[64,128]{1,0:T(8,128)}, u32[]{:S(2)}) copy-start(s32[64,128]{1,0:T(8,128)} %order_hbm.1) | copy-start | bytes 98308
  31.8 12.7 %copy-start.3 = (s32[62]{0:T(128)S(1)}, s32[62]{0:T(128)}, u32[]{:S(2)}) copy-start(s32[62]{0:T(128)} %cross_flags.1) | copy-start | bytes 748
  31.8 12.7 %copy-start.4 = (s32[1,63]{1,0:T(1,128)S(1)}, s32[1,63]{1,0:T(1,128)}, u32[]{:S(2)}) copy-start(s32[1,63]{1,0:T(1,128)} %flags.1) | copy-start | bytes 760
  37.7 12.7 %collective-permute-start.5 = (f32[8,2048]{1,0:T(8,128)S(1)}, f32[8,2048]{1,0:T(8,128)S(1)}, u32[]{:S(2)}, u32[]{:S(2)}) collective-permute-start(f32[8,2048]{1,0:T(8,128)S(1)} %get-tuple-element.28), channel_id=1, source_target_pairs={{0,3},{1,0},{2,1},{3,2},{4,7},{5,4},{6,5},{7,6},{8,11},{9,8},{10,9... | collective-permute-start | bytes 196616 | tf_op jit(solution)/shard_map/ppermute | solution.py:321
  38.1 12.3 %collective-permute-start.6 = (f32[8,2048]{1,0:T(8,128)S(1)}, f32[8,2048]{1,0:T(8,128)S(1)}, u32[]{:S(2)}, u32[]{:S(2)}) collective-permute-start(f32[8,2048]{1,0:T(8,128)S(1)} %get-tuple-element.29), channel_id=1, source_target_pairs={{0,2},{1,3},{2,0},{3,1},{4,6},{5,7},{6,4},{7,5},{8,10},{9,11},{10,... | collective-permute-start | bytes 196616 | tf_op jit(solution)/shard_map/ppermute | solution.py:321
  40.9 9.4 %collective-permute-start.7 = (f32[8,2048]{1,0:T(8,128)S(1)}, f32[8,2048]{1,0:T(8,128)S(1)}, u32[]{:S(2)}, u32[]{:S(2)}) collective-permute-start(f32[8,2048]{1,0:T(8,128)S(1)} %get-tuple-element.30), channel_id=1, source_target_pairs={{0,1},{1,2},{2,3},{3,0},{4,5},{5,6},{6,7},{7,4},{8,9},{9,10},{10,1... | collective-permute-start | bytes 196616 | tf_op jit(solution)/shard_map/ppermute | solution.py:321

commit v3 on v2

--- a/solution.py
+++ b/solution.py
@@ -9,7 +9,10 @@
 
 W = 8
 NEAR_US = 5
-EARLY = 1
+EARLY = 0
+CHUNKS = 2
+MCHUNKS = 1
+UNROLL = 4
 MIB = 52
 MIB0 = 52
 ROOT_HALF = 1.0 / math.sqrt(2.0)
@@ -65,35 +68,34 @@
     return jnp.take_along_axis(x, index, axis=1, mode="promise_in_bounds")
 
 
-def order_kernel(panels_hbm, order_hbm, middle, head, tail, panels, order, sems):
+def order_kernel(panels_hbm, order_hbm, middle, near_rim, far_rim, panels, order, sems):
     copies = [
         pltpu.make_async_copy(order_hbm, order, sems.at[0]),
         pltpu.make_async_copy(panels_hbm, panels, sems.at[1]),
     ]
+    even = (lax.axis_index("leaf") & 1) == 0
     for copy in copies:
         copy.start()
     for copy in copies:
         copy.wait()
     leaves = order.shape[0]
+    first, last = [], []
     for i in range(leaves):
+        at = slice(128 * i, 128 * (i + 1))
         index = jnp.broadcast_to(order[i : i + 1, :], (panels.shape[0], 128))
-        placed = lane_gather(panels[:, 128 * i : 128 * (i + 1)], index)
+        placed = lane_gather(panels[:, at], index)
         middle[:, 128 * (i + W) : 128 * (i + W + 1)] = placed
         if i < W:
-            head[:, 128 * i : 128 * (i + 1)] = placed
+            first.append(placed)
         if i >= leaves - W:
-            j = i - (leaves - W)
-            tail[:, 128 * j : 128 * (j + 1)] = placed
-
-
-def rim_kernel(middle, before, after, extended):
-    del middle
-    width = before.shape[1]
-    extended[:, :width] = before[...]
-    extended[:, extended.shape[1] - width :] = after[...]
-
-
-def inverse_kernel(order, inverse):
+            last.append(placed)
+    for i in range(W):
+        at = slice(128 * i, 128 * (i + 1))
+        near_rim[:, at] = jnp.where(even, last[i], first[i])
+        far_rim[:, at] = jnp.where(even, first[i], last[i])
+
+
+def invert(order, inverse):
     leaves = order.shape[0]
     rows = lax.broadcasted_iota(jnp.int32, (128, 128), 0)
     places = lax.broadcasted_iota(jnp.int32, (16, 128), 1).astype(F32).astype(BF16)
@@ -103,14 +105,17 @@
         inverse[i : i + 1, :] = inv[0:1].astype(jnp.int32)
 
 
-def up_kernel(middle, basis_hbm, mats_hbm, pairs, packets, basis, mats, basis_sems, mats_sems):
+def up_kernel(
+    middle, near_rim, order, basis_hbm, mats_hbm, pairs, packet, inverse, basis, mats, basis_sems, mats_sems
+):
     leaves = basis.shape[0]
     rank = basis.shape[1]
     count = leaves // 2
     nodes = []
     chunks = basis_sems.shape[0]
     basis_copies = chunked(basis_hbm, basis, basis_sems, chunks)
-    mats_copies = chunked(mats_hbm, mats, mats_sems, 2)
+    mats_copies = chunked(mats_hbm, mats, mats_sems, mats_sems.shape[0])
+    invert(order, inverse)
     for j in range(count):
         if j % (count // chunks) == 0:
             basis_copies[j // (count // chunks)].wait()
@@ -120,7 +125,7 @@
     first_pair, first_node = 0, 0
     mats_copies[0].wait()
     while count > 1:
-        if first_node == leaves // 2:
+        if first_node == leaves // 2 and len(mats_copies) == 2:
             mats_copies[1].wait()
         lifted = []
         for j in range(count // 2):
@@ -135,8 +140,23 @@
         count //= 2
     skel = nodes[0]
     lift = mul_nn(skel, mats[first_node])[:, rank:]
-    packet = jnp.concatenate([skel, lift], axis=1)
-    packets[...] = jnp.broadcast_to(packet[None], packets.shape)
+    packet[:, : near_rim.shape[1]] = near_rim[...]
+    packet[:, near_rim.shape[1] :] = jnp.concatenate([skel, lift], axis=1)
+
+
+def join_kernel(middle, packet, other, far_rim, extended, packets):
+    del middle
+    even = (lax.axis_index("leaf") & 1) == 0
+    width = far_rim.shape[1]
+    near_rim = other[:, :width]
+    extended[:, :width] = jnp.where(even, far_rim[...], near_rim)
+    extended[:, extended.shape[1] - width :] = jnp.where(even, near_rim, far_rim[...])
+    half = packets.shape[1]
+    rank = packets.shape[2] // 2
+    lift = width + rank
+    node = (packet[:, lift:] + other[:, lift:]) * ROOT_HALF
+    rows = jnp.concatenate([node[:half], node[half:]], axis=1)
+    packets[...] = jnp.broadcast_to(rows[None], packets.shape)
 
 
 def near_kernel(cols, own, arr1, arr2, arr3, tiles_hbm, out0, out1, out2, out3, held, tiles, sems):
@@ -175,18 +195,19 @@
     quarter = leaves // 16
     for c in range(4):
         copies[c].wait()
-        lax.fori_loop(c * quarter, (c + 1) * quarter, group, 0, unroll=2)
+        lax.fori_loop(c * quarter, (c + 1) * quarter, group, 0, unroll=UNROLL)
 
 
 def down_kernel(
-    cross_flags, flags, packets, pairs, basis_hbm, mats_hbm, coupling_hbm, transfer_hbm,
+    cross_flags, flags, packets, other, pairs, basis_hbm, mats_hbm, coupling_hbm, transfer_hbm,
     far, skels, basis, mats, coupling, transfer, sems,
 ):
     leaves = basis.shape[0]
     rank = basis.shape[1]
-    devices = packets.shape[0]
+    devices = 2 * packets.shape[0]
     depth = devices.bit_length() - 1
     me = lax.axis_index("leaf")
+    skel = other.shape[1] - 2 * rank
     transfer_copy = pltpu.make_async_copy(transfer_hbm, transfer, sems.at[0])
     transfer_copy.start()
     coupling_copies = []
@@ -202,7 +223,7 @@
     basis_copy.start()
     count = devices // 2
     nodes = [
-        (packets[2 * j][:, rank:] + packets[2 * j + 1][:, rank:]) * ROOT_HALF for j in range(count)
+        jnp.concatenate([packets[j][:, :rank], packets[j][:, rank:]], axis=0) for j in range(count)
     ]
     first = 0
     transfer_copy.wait()
@@ -233,7 +254,7 @@
         else:
             z = mul_nt(x, w) + mul_nt(z, transfer[node])
     top = leaves - 2
-    x = jnp.concatenate([packets[me ^ 1][:, :rank] * flags[0, top].astype(F32), z], axis=1)
+    x = jnp.concatenate([other[:, skel : skel + rank] * flags[0, top].astype(F32), z], axis=1)
     mats_copy.wait()
     zs = [mul_nt(x, mats[top])]
     count = 2
@@ -258,10 +279,12 @@
         far[:, 256 * j : 256 * (j + 1)] = both
 
 
-def final_kernel(inverse, far, near0, near1, near2, near3, out):
+def final_kernel(inverse, far, near0, near1, near2, near3, out_hbm, out, sems):
     leaves = inverse.shape[0]
     me = lax.axis_index("vec")
     nears = (near0, near1, near2, near3)
+    copies = []
+    chunk = leaves // sems.shape[0]
     for i in range(leaves):
         index = jnp.broadcast_to(inverse[i : i + 1, :], (out.shape[0], 128))
         owner = ((index >> 5) - me) & 3
@@ -272,15 +295,22 @@
             near = jnp.where(owner == k, lane_gather(nears[k][:, at], place), near)
         spot = slice(128 * i, 128 * (i + 1))
         out[:, spot] = near + lane_gather(far[:, spot], index)
-
-
-def call(kernel, spaces, ins, out_shapes, scratch=(), mib=0, us=0, alias={}):
+        if (i + 1) % chunk == 0:
+            c = i // chunk
+            at = pl.ds(128 * chunk * c, 128 * chunk)
+            copies.append(pltpu.make_async_copy(out.at[:, at], out_hbm.at[:, at], sems.at[c]))
+            copies[-1].start()
+    for copy in copies:
+        copy.wait()
+
+
+def call(kernel, spaces, ins, out_shapes, scratch=(), mib=0, us=0, out_space=vmem, alias={}):
     place = {"s": smem, "v": vmem, "h": hbm}
     return pl.pallas_call(
         kernel,
         out_shape=[jax.ShapeDtypeStruct(s, t) for s, t in out_shapes],
         in_specs=[place[k]() for k in spaces],
-        out_specs=[vmem()] * len(out_shapes),
+        out_specs=[out_space()] * len(out_shapes),
         scratch_shapes=list(scratch),
         input_output_aliases=alias,
         compiler_params=params(mib or MIB),
@@ -322,19 +352,10 @@
 
     dma = pltpu.SemaphoreType.DMA
 
-    def up(source):
-        return call(
-            up_kernel,
-            "vhh",
-            (source, leaf_basis, mats),
-            [((leaves // 2 - 1, rhs, 2 * rank), F32), ((devices, rhs, 2 * rank), F32)],
-            [basis_shape, mats_shape, dma((8,)), dma((2,))],
-        )
-
     basis_shape = pltpu.VMEM(leaf_basis.shape, F32)
     mats_shape = pltpu.VMEM(mats.shape, F32)
     length = (leaves + 2 * W) * size
-    middle, head, tail = call(
+    middle, near_rim, far_rim = call(
         order_kernel,
         "hh",
         (panels, leaf_order),
@@ -342,20 +363,34 @@
         [pltpu.VMEM(panels.shape, F32), pltpu.VMEM(leaf_order.shape, jnp.int32), dma((2,))],
         MIB0,
     )
-    ends = devices - 1
-    before = lax.ppermute(tail, "leaf", [(i, i + 1) for i in range(ends)])
-    after = lax.ppermute(head, "leaf", [(i + 1, i) for i in range(ends)])
-    (inverse,) = call(inverse_kernel, "v", (leaf_order,), [((leaves, size), jnp.int32)])
+    across = [(i, i + 1) for i in range(1, devices - 1, 2)]
+    far_rim = lax.ppermute(far_rim, "leaf", across + [(j, i) for i, j in across])
+    pairs, packet, inverse = call(
+        up_kernel,
+        "vvvhh",
+        (middle, near_rim, leaf_order, leaf_basis, mats),
+        [
+            ((leaves // 2 - 1, rhs, 2 * rank), F32),
+            ((rhs, rim + 2 * rank), F32),
+            ((leaves, size), jnp.int32),
+        ],
+        [basis_shape, mats_shape, dma((CHUNKS,)), dma((MCHUNKS,))],
+    )
     if EARLY:
-        pairs, packets = up(middle)
-        middle, before, after, packets = lax.optimization_barrier((middle, before, after, packets))
-    if EARLY == 2:
-        middle, before, after, inverse = lax.optimization_barrier((middle, before, after, inverse))
-    (own,) = call(rim_kernel, "vvv", (middle, before, after), [((rhs, length), F32)], alias={0: 0})
+        packet, far_rim = lax.optimization_barrier((packet, far_rim))
+    other = lax.ppermute(packet, "leaf", [(i, i ^ 1) for i in range(devices)])
+    chips = devices // 2
+    own, packets = call(
+        join_kernel,
+        "vvvv",
+        (middle, packet, other, far_rim),
+        [((rhs, length), F32), ((chips, rhs // 2, 2 * rank), F32)],
+        alias={0: 0},
+    )
     others = [turned(own, k) for k in (1, 2, 3)]
-    if not EARLY:
-        pairs, packets = up(own)
-    gathered = lax.all_to_all(packets, "leaf", 0, 0)
+    groups = [[core + 2 * i for i in range(chips)] for core in (0, 1)]
+    gathered = lax.all_to_all(packets, "leaf", 0, 0, axis_index_groups=groups)
+
     near = call(
         near_kernel,
         "svvvvh",
@@ -373,8 +408,8 @@
 
     (far,) = call(
         down_kernel,
-        "ssvvhhhh",
-        (cross_flags, local_flags, gathered, pairs, leaf_basis, mats, cross_coupling, cross_transfer),
+        "ssvvvhhhh",
+        (cross_flags, local_flags, gathered, other, pairs, leaf_basis, mats, cross_coupling, cross_transfer),
         [((rhs, leaves * size), F32)],
         [
             pltpu.VMEM((devices - 2, rhs, rank), F32),
@@ -385,7 +420,14 @@
             dma((devices.bit_length() + 2,)),
         ],
     )
-    (out,) = call(final_kernel, "vvvvvv", (inverse, far, *back), [((rhs, leaves * size), F32)])
+    (out,) = call(
+        final_kernel,
+        "vvvvvv",
+        (inverse, far, *back),
+        [((rhs, leaves * size), F32)],
+        [pltpu.VMEM(panels.shape, F32), dma((4,))],
+        out_space=hbm,
+    )
     return out
 
 

time: 52.1 us -> 47.8 us (0.917)
  the two profiles are of different devices: /device:TPU:112 before, /device:TPU:2 now
where the time goes in v3:
time: 47.8 us; the launch traced here: 46.9 us
  starting transfers between devices  26.4 us (55%)
  Pallas kernels  16.1 us (34%)
  waiting for transfers between devices  2.55 us (5%)
  local copies, waits for them, and re-layouts  1.72 us (4%)
    pallas_call x6, Pallas kernels, call(): pl.pallas_call(kernel, out_shape=[jax.ShapeDtypeStruct(s, t) for s, t in...  16.1 us
    ppermute x6, starting transfers between devices, turned(): return lax.ppermute(x, 'vec', [(i, (i + k) % parts) for i in range(parts)])  9.87 us
    all_to_all x1, starting transfers between devices, local(): gathered = lax.all_to_all(packets, 'leaf', 0, 0, axis_index_groups=groups)  8.65 us
    ppermute x1, starting transfers between devices, local(): lax.ppermute(far_rim, 'leaf', across + [(j, i) for i, j in across])  7.83 us
    unnamed x10, local copies, waits for them, and re-layouts  1.72 us
    ppermute x1, waiting for transfers between devices, local(): lax.ppermute(far_rim, 'leaf', across + [(j, i) for i, j in across])  1.58 us
    ppermute x6, waiting for transfers between devices, turned(): return lax.ppermute(x, 'vec', [(i, (i + k) % parts) for i in range(parts)])  0.96 us
  transfers between devices with their start and end apart: 9, of which 2 were waited for; matrix products, arithmetic and copies ran while one was open for 0% of the time, Pallas kernels for 22%

profile of v3, /device:TPU:2, one launch (start us, length us, event | category | flops | bytes accessed | tf_op | source)
XLA Modules:
  0.0 46.9 jit_solution(15745820007012668)
XLA Ops:
  0.0 0.0 copy-start
  0.0 0.9 %copy-done = f32[8,8192]{1,0:T(8,128)S(1)} copy-done((f32[8,8192]{1,0:T(8,128)S(1)}, f32[8,8192]{1,0:T(8,128)}, u32[]{:S(2)}) %copy-start) | copy-done | bytes 262168
  1.0 0.0 copy-start.1
  1.0 0.8 %copy-done.1 = s32[64,128]{1,0:T(8,128)S(1)} copy-done((s32[64,128]{1,0:T(8,128)S(1)}, s32[64,128]{1,0:T(8,128)}, u32[]{:S(2)}) %copy-start.1) | copy-done | bytes 32792
  1.7 0.3 shard_map.100
  2.0 0.0 copy-start.4
  2.0 3.4 %shard_map.101 = (f32[31,8,128]{2,1,0:T(8,128)S(1)}, f32[8,1152]{1,0:T(8,128)S(1)}, s32[64,128]{1,0:T(8,128)S(1)}) custom-call(f32[8,10240]{1,0:T(8,128)S(1)} %get-tuple-element.17.middle, f32[8,1024]{1,0:T(8,128)S(1)} %get-tuple-element.18.near_rim, s32[64,128]{1,0:T(8,128)S(1)} %copy-done.1, f32[64,64,128]{2,1,0:T(8,128)} %basis_hbm.3, f32[63,64,128]{2,1,0:T(8,128)} %bitcast.3), custom_call_target="tpu_custom_call" | custom-call | tf_op jit(solution)/shard_map/pallas_call | solution.py:309
  5.4 0.1 collective-permute-start
  5.5 7.8 %collective-permute-start.1 = (f32[8,1024]{1,0:T(8,128)S(1)}, f32[8,1024]{1,0:T(8,128)S(1)}, u32[]{:S(2)}, u32[]{:S(2)}) collective-permute-start(f32[8,1024]{1,0:T(8,128)S(1)} %get-tuple-element.21), channel_id=1, source_target_pairs={{4,8},{12,16},{20,24},{28,32},{36,40},{44,48},{52,56},{60,64},{68,... | collective-permute-start | bytes 98312 | tf_op jit(solution)/shard_map/ppermute | solution.py:367
  13.4 1.6 %collective-permute-done.1.far_rim = f32[8,1024]{1,0:T(8,128)S(1)} collective-permute-done((f32[8,1024]{1,0:T(8,128)S(1)}, f32[8,1024]{1,0:T(8,128)S(1)}, u32[]{:S(2)}, u32[]{:S(2)}) %collective-permute-start.1) | collective-permute-done | bytes 32800 | tf_op jit(solution)/shard_map/ppermute | solution.py:367
  14.9 0.0 collective-permute-done.other
  14.9 0.7 %shard_map.102 = (f32[8,10240]{1,0:T(8,128)S(1)}, f32[32,4,128]{2,1,0:T(4,128)}) custom-call(f32[8,10240]{1,0:T(8,128)S(1)} %get-tuple-element.17.middle, f32[8,1152]{1,0:T(8,128)S(1)} %get-tuple-element.20.packet, f32[8,1152]{1,0:T(8,128)S(1)} %collective-permute-done.other, ...), custom_call_target="tpu_custom_call", output_to_operand_aliasing={{0}: (0, {})} | custom-call | tf_op jit(solution)/shard_map/pallas_call | solution.py:309
  15.7 1.6 %collective-permute-start.2 = (f32[8,10240]{1,0:T(8,128)S(1)}, f32[8,10240]{1,0:T(8,128)S(1)}, u32[]{:S(2)}, u32[]{:S(2)}) collective-permute-start(f32[8,10240]{1,0:T(8,128)S(1)} %get-tuple-element.24.own), channel_id=1, source_target_pairs={{0,1},{1,2},{2,3},{3,0},{4,5},{5,6},{6,7},{7,4},{8,9},{9,10},{10,1... | collective-permute-start | bytes 983048 | tf_op jit(solution)/shard_map/ppermute | solution.py:351
  17.2 2.9 %collective-permute-start.3 = (f32[8,10240]{1,0:T(8,128)S(1)}, f32[8,10240]{1,0:T(8,128)S(1)}, u32[]{:S(2)}, u32[]{:S(2)}) collective-permute-start(f32[8,10240]{1,0:T(8,128)S(1)} %get-tuple-element.24.own), channel_id=1, source_target_pairs={{0,2},{1,3},{2,0},{3,1},{4,6},{5,7},{6,4},{7,5},{8,10},{9,11},{10,... | collective-permute-start | bytes 983048 | tf_op jit(solution)/shard_map/ppermute | solution.py:351
  20.1 1.3 %collective-permute-start.4 = (f32[8,10240]{1,0:T(8,128)S(1)}, f32[8,10240]{1,0:T(8,128)S(1)}, u32[]{:S(2)}, u32[]{:S(2)}) collective-permute-start(f32[8,10240]{1,0:T(8,128)S(1)} %get-tuple-element.24.own), channel_id=1, source_target_pairs={{0,3},{1,0},{2,1},{3,2},{4,7},{5,4},{6,5},{7,6},{8,11},{9,8},{10,9... | collective-permute-start | bytes 983048 | tf_op jit(solution)/shard_map/ppermute | solution.py:351
  21.5 8.6 %all-to-all-start = ((f32[32,4,128]{2,1,0:T(4,128)}), f32[32,4,128]{2,1,0:T(4,128)S(1)}, u32[]{:S(2)}, u32[]{:S(2)}) async-start(f32[32,4,128]{2,1,0:T(4,128)} %get-tuple-element.22), calls=%async_computation | async-start | bytes 131072 | tf_op jit(solution)/shard_map/all_to_all | solution.py:392
  30.1 0.0 collective-permute-done.2.arr1
  30.2 0.9 %collective-permute-done.3.arr2 = f32[8,10240]{1,0:T(8,128)S(1)} collective-permute-done((f32[8,10240]{1,0:T(8,128)S(1)}, f32[8,10240]{1,0:T(8,128)S(1)}, u32[]{:S(2)}, u32[]{:S(2)}) %collective-permute-start.3) | collective-permute-done | bytes 327712 | tf_op jit(solution)/shard_map/ppermute | solution.py:351
  31.1 0.0 collective-permute-done.4.arr3
  31.1 0.0 copy-done.4
  31.1 0.0 copy-start.2
  31.1 0.0 copy-start.3
  31.1 4.4 %shard_map.104 = (f32[8,2048]{1,0:T(8,128)S(1)}, f32[8,2048]{1,0:T(8,128)S(1)}, f32[8,2048]{1,0:T(8,128)S(1)}, f32[8,2048]{1,0:T(8,128)S(1)}) custom-call(s32[4,64]{1,0:T(4,128)S(1)} %bitcast.2, f32[8,10240]{1,0:T(8,128)S(1)} %get-tuple-element.24.own, f32[8,10240]{1,0:T(8,128)S(1)} %collective-permute-done.2.arr1, ...), custom_call_target="tpu_custom_call" | custom-call | flops 5750000128 | tf_op jit(solution)/shard_map/pallas_call | solution.py:309
  35.5 2.1 %collective-permute-start.5 = (f32[8,2048]{1,0:T(8,128)S(1)}, f32[8,2048]{1,0:T(8,128)S(1)}, u32[]{:S(2)}, u32[]{:S(2)}) collective-permute-start(f32[8,2048]{1,0:T(8,128)S(1)} %get-tuple-element.26), channel_id=1, source_target_pairs={{0,3},{1,0},{2,1},{3,2},{4,7},{5,4},{6,5},{7,6},{8,11},{9,8},{10,9... | collective-permute-start | bytes 196616 | tf_op jit(solution)/shard_map/ppermute | solution.py:351
  37.6 1.1 %collective-permute-start.6 = (f32[8,2048]{1,0:T(8,128)S(1)}, f32[8,2048]{1,0:T(8,128)S(1)}, u32[]{:S(2)}, u32[]{:S(2)}) collective-permute-start(f32[8,2048]{1,0:T(8,128)S(1)} %get-tuple-element.27), channel_id=1, source_target_pairs={{0,2},{1,3},{2,0},{3,1},{4,6},{5,7},{6,4},{7,5},{8,10},{9,11},{10,... | collective-permute-start | bytes 196616 | tf_op jit(solution)/shard_map/ppermute | solution.py:351
  38.7 0.8 %collective-permute-start.7 = (f32[8,2048]{1,0:T(8,128)S(1)}, f32[8,2048]{1,0:T(8,128)S(1)}, u32[]{:S(2)}, u32[]{:S(2)}) collective-permute-start(f32[8,2048]{1,0:T(8,128)S(1)} %get-tuple-element.28), channel_id=1, source_target_pairs={{0,1},{1,2},{2,3},{3,0},{4,5},{5,6},{6,7},{7,4},{8,9},{9,10},{10,1... | collective-permute-start | bytes 196616 | tf_op jit(solution)/shard_map/ppermute | solution.py:351
  39.5 0.0 all-to-all-done.packets
  39.5 0.0 copy-done.2
  39.5 0.0 copy-done.3
  39.5 5.9 %shard_map.103.far = f32[8,8192]{1,0:T(8,128)S(1)} custom-call(s32[62]{0:T(128)S(1)} %copy-done.2, s32[1,63]{1,0:T(1,128)S(1)} %copy-done.3, f32[32,4,128]{2,1,0:T(4,128)S(1)} %all-to-all-done.packets, f32[8,1152]{1,0:T(8,128)S(1)} %collective-permute-done.other, f32[31,8,128]{2,1,0:T(8,128)S(1)} %get-tuple-element.23.pairs, f32[64,64,128]{2,1,0:T(8,128)} %basis_hbm.3, ...), custom_call_target="tpu_custom_call" | custom-call | tf_op jit(solution)/shard_map/pallas_call | solution.py:309
  45.4 0.0 collective-permute-done.5.near1
  45.4 0.0 collective-permute-done.6.near2
  45.5 0.0 collective-permute-done.7.near3
  45.5 1.4 %shard_map.105 = f32[8,8192]{1,0:T(8,128)} custom-call(s32[64,128]{1,0:T(8,128)S(1)} %get-tuple-element.19.inverse, f32[8,8192]{1,0:T(8,128)S(1)} %shard_map.103.far, f32[8,2048]{1,0:T(8,128)S(1)} %get-tuple-element.25.near0, f32[8,2048]{1,0:T(8,128)S(1)} %collective-permute-done.5.near1, f32[8,2048]{1,0:T(8,128)S(1)} %collective-permute-done.6.near2, ...), custom_call_target="tpu_custom_call" | custom-call | tf_op jit(solution)/shard_map/pallas_call | solution.py:309
Async XLA Ops:
  0.0 0.9 %copy-start = (f32[8,8192]{1,0:T(8,128)S(1)}, f32[8,8192]{1,0:T(8,128)}, u32[]{:S(2)}) copy-start(f32[8,8192]{1,0:T(8,128)} %panels_hbm.1) | copy-start | bytes 786436
  1.0 0.8 %copy-start.1 = (s32[64,128]{1,0:T(8,128)S(1)}, s32[64,128]{1,0:T(8,128)}, u32[]{:S(2)}) copy-start(s32[64,128]{1,0:T(8,128)} %order.1) | copy-start | bytes 98308
  2.0 29.1 %copy-start.4 = (s32[64,4]{0,1:T(4,128)S(1)}, s32[64,4]{0,1:T(4,128)}, u32[]{:S(2)}) copy-start(s32[64,4]{0,1:T(4,128)} %param.12) | copy-start | bytes 3076
  5.4 9.5 %collective-permute-start = (f32[8,1152]{1,0:T(8,128)S(1)}, f32[8,1152]{1,0:T(8,128)S(1)}, u32[]{:S(2)}, u32[]{:S(2)}) collective-permute-start(f32[8,1152]{1,0:T(8,128)S(1)} %get-tuple-element.20.packet), channel_id=1, source_target_pairs={{0,4},{4,0},{8,12},{12,8},{16,20},{20,16},{24,28},{28,24},{32,36},... | collective-permute-start | bytes 110600 | tf_op jit(solution)/shard_map/ppermute | solution.py:381
  5.5 9.4 %collective-permute-start.1 = (f32[8,1024]{1,0:T(8,128)S(1)}, f32[8,1024]{1,0:T(8,128)S(1)}, u32[]{:S(2)}, u32[]{:S(2)}) collective-permute-start(f32[8,1024]{1,0:T(8,128)S(1)} %get-tuple-element.21), channel_id=1, source_target_pairs={{4,8},{12,16},{20,24},{28,32},{36,40},{44,48},{52,56},{60,64},{68,... | collective-permute-start | bytes 98312 | tf_op jit(solution)/shard_map/ppermute | solution.py:367
  15.7 14.5 %collective-permute-start.2 = (f32[8,10240]{1,0:T(8,128)S(1)}, f32[8,10240]{1,0:T(8,128)S(1)}, u32[]{:S(2)}, u32[]{:S(2)}) collective-permute-start(f32[8,10240]{1,0:T(8,128)S(1)} %get-tuple-element.24.own), channel_id=1, source_target_pairs={{0,1},{1,2},{2,3},{3,0},{4,5},{5,6},{6,7},{7,4},{8,9},{9,10},{10,1... | collective-permute-start | bytes 983048 | tf_op jit(solution)/shard_map/ppermute | solution.py:351
  17.2 13.9 %collective-permute-start.3 = (f32[8,10240]{1,0:T(8,128)S(1)}, f32[8,10240]{1,0:T(8,128)S(1)}, u32[]{:S(2)}, u32[]{:S(2)}) collective-permute-start(f32[8,10240]{1,0:T(8,128)S(1)} %get-tuple-element.24.own), channel_id=1, source_target_pairs={{0,2},{1,3},{2,0},{3,1},{4,6},{5,7},{6,4},{7,5},{8,10},{9,11},{10,... | collective-permute-start | bytes 983048 | tf_op jit(solution)/shard_map/ppermute | solution.py:351
  20.1 11.0 %collective-permute-start.4 = (f32[8,10240]{1,0:T(8,128)S(1)}, f32[8,10240]{1,0:T(8,128)S(1)}, u32[]{:S(2)}, u32[]{:S(2)}) collective-permute-start(f32[8,10240]{1,0:T(8,128)S(1)} %get-tuple-element.24.own), channel_id=1, source_target_pairs={{0,3},{1,0},{2,1},{3,2},{4,7},{5,4},{6,5},{7,6},{8,11},{9,8},{10,9... | collective-permute-start | bytes 983048 | tf_op jit(solution)/shard_map/ppermute | solution.py:351
  21.5 18.1 %all-to-all-start = ((f32[32,4,128]{2,1,0:T(4,128)}), f32[32,4,128]{2,1,0:T(4,128)S(1)}, u32[]{:S(2)}, u32[]{:S(2)}) async-start(f32[32,4,128]{2,1,0:T(4,128)} %get-tuple-element.22), calls=%async_computation | async-start | bytes 131072 | tf_op jit(solution)/shard_map/all_to_all | solution.py:392
  31.1 8.4 %copy-start.2 = (s32[62]{0:T(128)S(1)}, s32[62]{0:T(128)}, u32[]{:S(2)}) copy-start(s32[62]{0:T(128)} %cross_flags.1) | copy-start | bytes 748
  31.1 8.4 %copy-start.3 = (s32[1,63]{1,0:T(1,128)S(1)}, s32[1,63]{1,0:T(1,128)}, u32[]{:S(2)}) copy-start(s32[1,63]{1,0:T(1,128)} %flags.1) | copy-start | bytes 760
  35.5 10.0 %collective-permute-start.5 = (f32[8,2048]{1,0:T(8,128)S(1)}, f32[8,2048]{1,0:T(8,128)S(1)}, u32[]{:S(2)}, u32[]{:S(2)}) collective-permute-start(f32[8,2048]{1,0:T(8,128)S(1)} %get-tuple-element.26), channel_id=1, source_target_pairs={{0,3},{1,0},{2,1},{3,2},{4,7},{5,4},{6,5},{7,6},{8,11},{9,8},{10,9... | collective-permute-start | bytes 196616 | tf_op jit(solution)/shard_map/ppermute | solution.py:351
  37.6 7.9 %collective-permute-start.6 = (f32[8,2048]{1,0:T(8,128)S(1)}, f32[8,2048]{1,0:T(8,128)S(1)}, u32[]{:S(2)}, u32[]{:S(2)}) collective-permute-start(f32[8,2048]{1,0:T(8,128)S(1)} %get-tuple-element.27), channel_id=1, source_target_pairs={{0,2},{1,3},{2,0},{3,1},{4,6},{5,7},{6,4},{7,5},{8,10},{9,11},{10,... | collective-permute-start | bytes 196616 | tf_op jit(solution)/shard_map/ppermute | solution.py:351
  38.7 6.8 %collective-permute-start.7 = (f32[8,2048]{1,0:T(8,128)S(1)}, f32[8,2048]{1,0:T(8,128)S(1)}, u32[]{:S(2)}, u32[]{:S(2)}) collective-permute-start(f32[8,2048]{1,0:T(8,128)S(1)} %get-tuple-element.28), channel_id=1, source_target_pairs={{0,1},{1,2},{2,3},{3,0},{4,5},{5,6},{6,7},{7,4},{8,9},{9,10},{10,1... | collective-permute-start | bytes 196616 | tf_op jit(solution)/shard_map/ppermute | solution.py:351

commit v4 on v3

--- a/solution.py
+++ b/solution.py
@@ -9,9 +9,9 @@
 
 W = 8
 NEAR_US = 5
-EARLY = 0
+TIE = 1
+PATH_US = 0
 CHUNKS = 2
-MCHUNKS = 1
 UNROLL = 4
 MIB = 52
 MIB0 = 52
@@ -66,33 +66,6 @@
 
 def lane_gather(x, index):
     return jnp.take_along_axis(x, index, axis=1, mode="promise_in_bounds")
-
-
-def order_kernel(panels_hbm, order_hbm, middle, near_rim, far_rim, panels, order, sems):
-    copies = [
-        pltpu.make_async_copy(order_hbm, order, sems.at[0]),
-        pltpu.make_async_copy(panels_hbm, panels, sems.at[1]),
-    ]
-    even = (lax.axis_index("leaf") & 1) == 0
-    for copy in copies:
-        copy.start()
-    for copy in copies:
-        copy.wait()
-    leaves = order.shape[0]
-    first, last = [], []
-    for i in range(leaves):
-        at = slice(128 * i, 128 * (i + 1))
-        index = jnp.broadcast_to(order[i : i + 1, :], (panels.shape[0], 128))
-        placed = lane_gather(panels[:, at], index)
-        middle[:, 128 * (i + W) : 128 * (i + W + 1)] = placed
-        if i < W:
-            first.append(placed)
-        if i >= leaves - W:
-            last.append(placed)
-    for i in range(W):
-        at = slice(128 * i, 128 * (i + 1))
-        near_rim[:, at] = jnp.where(even, last[i], first[i])
-        far_rim[:, at] = jnp.where(even, first[i], last[i])
 
 
 def invert(order, inverse):
@@ -106,27 +79,55 @@
 
 
 def up_kernel(
-    middle, near_rim, order, basis_hbm, mats_hbm, pairs, packet, inverse, basis, mats, basis_sems, mats_sems
+    panels_hbm, order_hbm, basis_hbm, mats_hbm, middle, far_rim, pairs, packet, inverse,
+    panels, order, basis, mats, sems, basis_sems, mats_sems,
 ):
+    copies = [
+        pltpu.make_async_copy(order_hbm, order, sems.at[0]),
+        pltpu.make_async_copy(panels_hbm, panels, sems.at[1]),
+    ]
+    for copy in copies:
+        copy.start()
     leaves = basis.shape[0]
     rank = basis.shape[1]
     count = leaves // 2
-    nodes = []
     chunks = basis_sems.shape[0]
     basis_copies = chunked(basis_hbm, basis, basis_sems, chunks)
     mats_copies = chunked(mats_hbm, mats, mats_sems, mats_sems.shape[0])
+    even = (lax.axis_index("leaf") & 1) == 0
+    for copy in copies:
+        copy.wait()
+    for i in range(leaves):
+        index = jnp.broadcast_to(order[i : i + 1, :], (panels.shape[0], 128))
+        placed = lane_gather(panels[:, 128 * i : 128 * (i + 1)], index)
+        middle[:, 128 * (i + W) : 128 * (i + W + 1)] = placed
+    for i in range(W):
+        first = middle[:, 128 * (i + W) : 128 * (i + W + 1)]
+        last = middle[:, 128 * (i + leaves) : 128 * (i + leaves + 1)]
+        at = slice(128 * i, 128 * (i + 1))
+        packet[:, at] = jnp.where(even, last, first)
+        far_rim[:, at] = jnp.where(even, first, last)
     invert(order, inverse)
-    for j in range(count):
+    nodes = []
+    for j in range(0, count, 2):
         if j % (count // chunks) == 0:
             basis_copies[j // (count // chunks)].wait()
-        x = middle[:, 128 * (2 * j + W) : 128 * (2 * j + 2 + W)]
-        w = jnp.concatenate([basis[2 * j], basis[2 * j + 1]], axis=1)
-        nodes.append(mul_nt(x, w) * ROOT_HALF)
+        at = 128 * (2 * j + W)
+        x = jnp.concatenate([middle[:, at : at + 256], middle[:, at + 256 : at + 512]], axis=0)
+        w = jnp.concatenate(
+            [
+                jnp.concatenate([basis[2 * j], basis[2 * j + 1]], axis=1),
+                jnp.concatenate([basis[2 * j + 2], basis[2 * j + 3]], axis=1),
+            ],
+            axis=0,
+        )
+        both = mul_nt(x, w) * ROOT_HALF
+        half = both.shape[0] // 2
+        nodes += [both[:half, :rank], both[half:, rank:]]
     first_pair, first_node = 0, 0
-    mats_copies[0].wait()
+    for copy in mats_copies:
+        copy.wait()
     while count > 1:
-        if first_node == leaves // 2 and len(mats_copies) == 2:
-            mats_copies[1].wait()
         lifted = []
         for j in range(count // 2):
             pair = jnp.concatenate([nodes[2 * j], nodes[2 * j + 1]], axis=1)
@@ -140,8 +141,34 @@
         count //= 2
     skel = nodes[0]
     lift = mul_nn(skel, mats[first_node])[:, rank:]
-    packet[:, : near_rim.shape[1]] = near_rim[...]
-    packet[:, near_rim.shape[1] :] = jnp.concatenate([skel, lift], axis=1)
+    packet[:, far_rim.shape[1] :] = jnp.concatenate([skel, lift], axis=1)
+
+
+def path_kernel(
+    after, mats_hbm, coupling_hbm, transfer_hbm, path, own, coupling, transfer, sems
+):
+    del after
+    me = lax.axis_index("leaf")
+    levels = coupling.shape[0]
+    rank = own.shape[0]
+    copies = [pltpu.make_async_copy(mats_hbm.at[mats_hbm.shape[0] - 1], own, sems.at[0])]
+    for c in range(1, levels + 1):
+        node = (2 << levels) - (2 << levels >> (c - 1)) + (me >> c)
+        copies.append(pltpu.make_async_copy(coupling_hbm.at[node], coupling.at[c - 1], sems.at[2 * c - 1]))
+        if c < levels:
+            copies.append(pltpu.make_async_copy(transfer_hbm.at[node], transfer.at[c - 1], sems.at[2 * c]))
+    for copy in copies:
+        copy.start()
+    for copy in copies:
+        copy.wait()
+    down = own[:, rank:]
+    terms = [own[:, :rank]]
+    for c in range(levels):
+        terms.append(mul_nn(down, coupling[c]))
+        if c < levels - 1:
+            down = mul_nn(down, transfer[c])
+    for i in range(len(terms) // 2):
+        path[i] = jnp.concatenate([terms[2 * i], terms[2 * i + 1]], axis=1)
 
 
 def join_kernel(middle, packet, other, far_rim, extended, packets):
@@ -199,8 +226,8 @@
 
 
 def down_kernel(
-    cross_flags, flags, packets, other, pairs, basis_hbm, mats_hbm, coupling_hbm, transfer_hbm,
-    far, skels, basis, mats, coupling, transfer, sems,
+    cross_flags, flags, packets, other, pairs, path, basis_hbm, mats_hbm, transfer_hbm,
+    far, skels, basis, mats, transfer, sems,
 ):
     leaves = basis.shape[0]
     rank = basis.shape[1]
@@ -210,13 +237,6 @@
     skel = other.shape[1] - 2 * rank
     transfer_copy = pltpu.make_async_copy(transfer_hbm, transfer, sems.at[0])
     transfer_copy.start()
-    coupling_copies = []
-    for c in range(1, depth):
-        node = devices - (devices >> (c - 1)) + (me >> c)
-        coupling_copies.append(
-            pltpu.make_async_copy(coupling_hbm.at[node], coupling.at[c - 1], sems.at[2 + c])
-        )
-        coupling_copies[-1].start()
     mats_copy = pltpu.make_async_copy(mats_hbm, mats, sems.at[1])
     mats_copy.start()
     basis_copy = pltpu.make_async_copy(basis_hbm, basis, sems.at[2])
@@ -240,23 +260,19 @@
             nodes = lifted
         first += count
         count //= 2
-    for copy in coupling_copies:
-        copy.wait()
-    z = None
-    for c in range(depth - 1, 0, -1):
+    top = leaves - 2
+    terms = [other[:, skel : skel + rank] * flags[0, top].astype(F32)]
+    for c in range(1, depth):
         start = devices - (devices >> (c - 1))
         node = start + (me >> c)
         sibling = start + ((me >> c) ^ 1)
-        x = skels[sibling] * cross_flags[node].astype(F32)
-        w = coupling[c - 1]
-        if z is None:
-            z = mul_nt(x, w)
-        else:
-            z = mul_nt(x, w) + mul_nt(z, transfer[node])
-    top = leaves - 2
-    x = jnp.concatenate([other[:, skel : skel + rank] * flags[0, top].astype(F32), z], axis=1)
+        terms.append(skels[sibling] * cross_flags[node].astype(F32))
+    z = None
+    for i in range(len(terms) // 2):
+        part = mul_nt(jnp.concatenate([terms[2 * i], terms[2 * i + 1]], axis=1), path[i])
+        z = part if z is None else z + part
+    zs = [z]
     mats_copy.wait()
-    zs = [mul_nt(x, mats[top])]
     count = 2
     while count < leaves:
         first_node = leaves - 2 * count
@@ -265,11 +281,13 @@
         for j in range(count // 2):
             pair = pairs[first_pair + j]
             z = zs[j]
-            for side in (0, 1):
-                node = first_node + 2 * j + side
-                other = pair[:, rank:] if side == 0 else pair[:, :rank]
-                x = jnp.concatenate([other * flags[0, node].astype(F32), z], axis=1)
-                lower.append(mul_nt(x, mats[node]))
+            node = first_node + 2 * j
+            left = jnp.concatenate([pair[:, rank:] * flags[0, node].astype(F32), z], axis=1)
+            right = jnp.concatenate([pair[:, :rank] * flags[0, node + 1].astype(F32), z], axis=1)
+            w = mats[node : node + 2].reshape(2 * rank, 2 * rank)
+            both = mul_nt(jnp.concatenate([left, right], axis=0), w)
+            half = both.shape[0] // 2
+            lower += [both[:half, :rank], both[half:, rank:]]
         zs = lower
         count *= 2
     basis_copy.wait()
@@ -355,29 +373,31 @@
     basis_shape = pltpu.VMEM(leaf_basis.shape, F32)
     mats_shape = pltpu.VMEM(mats.shape, F32)
     length = (leaves + 2 * W) * size
-    middle, near_rim, far_rim = call(
-        order_kernel,
-        "hh",
-        (panels, leaf_order),
-        [((rhs, length), F32), ((rhs, rim), F32), ((rhs, rim), F32)],
-        [pltpu.VMEM(panels.shape, F32), pltpu.VMEM(leaf_order.shape, jnp.int32), dma((2,))],
-        MIB0,
-    )
-    across = [(i, i + 1) for i in range(1, devices - 1, 2)]
-    far_rim = lax.ppermute(far_rim, "leaf", across + [(j, i) for i, j in across])
-    pairs, packet, inverse = call(
+    levels = devices.bit_length() - 2
+    middle, far_rim, pairs, packet, inverse = call(
         up_kernel,
-        "vvvhh",
-        (middle, near_rim, leaf_order, leaf_basis, mats),
+        "hhhh",
+        (panels, leaf_order, leaf_basis, mats),
         [
+            ((rhs, length), F32),
+            ((rhs, rim), F32),
             ((leaves // 2 - 1, rhs, 2 * rank), F32),
             ((rhs, rim + 2 * rank), F32),
             ((leaves, size), jnp.int32),
         ],
-        [basis_shape, mats_shape, dma((CHUNKS,)), dma((MCHUNKS,))],
-    )
-    if EARLY:
-        packet, far_rim = lax.optimization_barrier((packet, far_rim))
+        [
+            pltpu.VMEM(panels.shape, F32),
+            pltpu.VMEM(leaf_order.shape, jnp.int32),
+            basis_shape,
+            mats_shape,
+            dma((2,)),
+            dma((CHUNKS,)),
+            dma((1,)),
+        ],
+        MIB0,
+    )
+    across = [(i, i + 1) for i in range(1, devices - 1, 2)]
+    far_rim = lax.ppermute(far_rim, "leaf", across + [(j, i) for i, j in across])
     other = lax.ppermute(packet, "leaf", [(i, i ^ 1) for i in range(devices)])
     chips = devices // 2
     own, packets = call(
@@ -391,10 +411,26 @@
     groups = [[core + 2 * i for i in range(chips)] for core in (0, 1)]
     gathered = lax.all_to_all(packets, "leaf", 0, 0, axis_index_groups=groups)
 
+    (path,) = call(
+        path_kernel,
+        "vhhh",
+        (other, mats, cross_coupling, cross_transfer),
+        [(((levels + 1) // 2, rank, 2 * rank), F32)],
+        [
+            pltpu.VMEM(mats.shape[1:], F32),
+            pltpu.VMEM((levels, rank, rank), F32),
+            pltpu.VMEM((levels - 1, rank, rank), F32),
+            dma((2 * levels,)),
+        ],
+        us=PATH_US,
+    )
+    cols = near_cols.T
+    if TIE:
+        cols, path = lax.optimization_barrier((cols, path))
     near = call(
         near_kernel,
         "svvvvh",
-        (near_cols.T, own, *others, near_tiles),
+        (cols, own, *others, near_tiles),
         [((rhs, leaves * near_tiles.shape[2]), F32)] * 4,
         [
             pltpu.VMEM((leaves + 2 * W, 2 * parts * rhs, size), BF16),
@@ -408,16 +444,15 @@
 
     (far,) = call(
         down_kernel,
-        "ssvvvhhhh",
-        (cross_flags, local_flags, gathered, other, pairs, leaf_basis, mats, cross_coupling, cross_transfer),
+        "ssvvvvhhh",
+        (cross_flags, local_flags, gathered, other, pairs, path, leaf_basis, mats, cross_transfer),
         [((rhs, leaves * size), F32)],
         [
             pltpu.VMEM((devices - 2, rhs, rank), F32),
             basis_shape,
             mats_shape,
-            pltpu.VMEM((devices.bit_length() - 2, rank, rank), F32),
             pltpu.VMEM(cross_transfer.shape, F32),
-            dma((devices.bit_length() + 2,)),
+            dma((3,)),
         ],
     )
     (out,) = call(

time: 47.8 us -> 47.4 us (level)
  the two profiles are of different devices: /device:TPU:2 before, /device:TPU:114 now
where the time goes in v4:
time: 47.4 us; the launch traced here: 47.1 us
  starting transfers between devices  22.6 us (48%)
  Pallas kernels  16.8 us (35%)
  waiting for transfers between devices  5.73 us (12%)
  local copies, waits for them, and re-layouts  1.73 us (4%)
    pallas_call x6, Pallas kernels, call(): pl.pallas_call(kernel, out_shape=[jax.ShapeDtypeStruct(s, t) for s, t in...  16.8 us
    all_to_all x1, starting transfers between devices, local(): gathered = lax.all_to_all(packets, 'leaf', 0, 0, axis_index_groups=groups)  11.5 us
    ppermute x6, starting transfers between devices, turned(): return lax.ppermute(x, 'vec', [(i, (i + k) % parts) for i in range(parts)])  8.96 us
    ppermute x1, waiting for transfers between devices, local(): lax.ppermute(far_rim, 'leaf', across + [(j, i) for i, j in across])  3.12 us
    ppermute x6, waiting for transfers between devices, turned(): return lax.ppermute(x, 'vec', [(i, (i + k) % parts) for i in range(parts)])  2.61 us
    ppermute x1, starting transfers between devices, local(): lax.ppermute(far_rim, 'leaf', across + [(j, i) for i, j in across])  2.11 us
    unnamed x10, local copies, waits for them, and re-layouts  1.73 us
  transfers between devices with their start and end apart: 9, of which 2 were waited for; matrix products, arithmetic and copies ran while one was open for 0% of the time, Pallas kernels for 24%

profile of v4, /device:TPU:114, one launch (start us, length us, event | category | flops | bytes accessed | tf_op | source)
XLA Modules:
  0.0 47.1 jit_solution(15640603290119058934)
XLA Ops:
  0.0 0.0 copy-start
  0.0 0.9 %copy-done = f32[8,8192]{1,0:T(8,128)S(1)} copy-done((f32[8,8192]{1,0:T(8,128)S(1)}, f32[8,8192]{1,0:T(8,128)}, u32[]{:S(2)}) %copy-start) | copy-done | bytes 262168
  1.0 0.0 copy-start.1
  1.0 0.8 %copy-done.1 = s32[64,128]{1,0:T(8,128)S(1)} copy-done((s32[64,128]{1,0:T(8,128)S(1)}, s32[64,128]{1,0:T(8,128)}, u32[]{:S(2)}) %copy-start.1) | copy-done | bytes 32792
  1.7 3.4 %shard_map.100 = (f32[8,10240]{1,0:T(8,128)S(1)}, f32[8,1024]{1,0:T(8,128)S(1)}, f32[31,8,128]{2,1,0:T(8,128)S(1)}, f32[8,1152]{1,0:T(8,128)S(1)}, s32[64,128]{1,0:T(8,128)S(1)}) custom-call(f32[8,8192]{1,0:T(8,128)S(1)} %copy-done, s32[64,128]{1,0:T(8,128)S(1)} %copy-done.1, f32[64,64,128]{2,1,0:T(8,128)} %basis_hbm.3, f32[63,64,128]{2,1,0:T(8,128)} %bitcast.3), custom_call_target="tpu_custom_call" | custom-call | tf_op jit(solution)/shard_map/pallas_call | solution.py:327
  5.1 0.1 collective-permute-start
  5.2 2.1 %collective-permute-start.1 = (f32[8,1024]{1,0:T(8,128)S(1)}, f32[8,1024]{1,0:T(8,128)S(1)}, u32[]{:S(2)}, u32[]{:S(2)}) collective-permute-start(f32[8,1024]{1,0:T(8,128)S(1)} %get-tuple-element.21), channel_id=1, source_target_pairs={{4,8},{12,16},{20,24},{28,32},{36,40},{44,48},{52,56},{60,64},{68,... | collective-permute-start | bytes 98312 | tf_op jit(solution)/shard_map/ppermute | solution.py:400
  7.3 3.1 %collective-permute-done.1.far_rim = f32[8,1024]{1,0:T(8,128)S(1)} collective-permute-done((f32[8,1024]{1,0:T(8,128)S(1)}, f32[8,1024]{1,0:T(8,128)S(1)}, u32[]{:S(2)}, u32[]{:S(2)}) %collective-permute-start.1) | collective-permute-done | bytes 32800 | tf_op jit(solution)/shard_map/ppermute | solution.py:400
  10.4 0.0 collective-permute-done.other.after
  10.4 0.7 %shard_map.101 = (f32[8,10240]{1,0:T(8,128)S(1)}, f32[32,4,128]{2,1,0:T(4,128)}) custom-call(f32[8,10240]{1,0:T(8,128)S(1)} %get-tuple-element.19.middle, f32[8,1152]{1,0:T(8,128)S(1)} %get-tuple-element.20.packet, f32[8,1152]{1,0:T(8,128)S(1)} %collective-permute-done.other.after, ...), custom_call_target="tpu_custom_call", output_to_operand_aliasing={{0}: (0, {})} | custom-call | tf_op jit(solution)/shard_map/pallas_call | solution.py:327
  11.2 0.4 collective-permute-start.4
  11.6 2.9 %collective-permute-start.3 = (f32[8,10240]{1,0:T(8,128)S(1)}, f32[8,10240]{1,0:T(8,128)S(1)}, u32[]{:S(2)}, u32[]{:S(2)}) collective-permute-start(f32[8,10240]{1,0:T(8,128)S(1)} %get-tuple-element.26.own), channel_id=1, source_target_pairs={{0,2},{1,3},{2,0},{3,1},{4,6},{5,7},{6,4},{7,5},{8,10},{9,11},{10,... | collective-permute-start | bytes 983048 | tf_op jit(solution)/shard_map/ppermute | solution.py:369
  14.5 0.0 collective-permute-start.2
  14.5 11.5 %all-to-all-start = ((f32[32,4,128]{2,1,0:T(4,128)}), f32[32,4,128]{2,1,0:T(4,128)S(1)}, u32[]{:S(2)}, u32[]{:S(2)}) async-start(f32[32,4,128]{2,1,0:T(4,128)} %get-tuple-element.22), calls=%async_computation | async-start | bytes 131072 | tf_op jit(solution)/shard_map/all_to_all | solution.py:412
  26.0 0.0 copy-start.4
  26.0 2.1 %shard_map.102.path = f32[3,64,128]{2,1,0:T(8,128)S(1)} custom-call(f32[8,1152]{1,0:T(8,128)S(1)} %collective-permute-done.other.after, f32[63,64,128]{2,1,0:T(8,128)} %bitcast.4, f32[62,64,64]{2,1,0:T(8,128)} %coupling_hbm.1, f32[60,64,64]{2,1,0:T(8,128)} %transfer_hbm.3), custom_call_target="tpu_custom_call" | custom-call | tf_op jit(solution)/shard_map/pallas_call | solution.py:327
  28.1 0.0 copy-start.2
  28.1 0.0 copy-start.3
  28.1 0.0 collective-permute-done.4.arr3
  28.1 0.0 collective-permute-done.3.arr2
  28.1 2.6 %collective-permute-done.2.arr1 = f32[8,10240]{1,0:T(8,128)S(1)} collective-permute-done((f32[8,10240]{1,0:T(8,128)S(1)}, f32[8,10240]{1,0:T(8,128)S(1)}, u32[]{:S(2)}, u32[]{:S(2)}) %collective-permute-start.2) | collective-permute-done | bytes 327712 | tf_op jit(solution)/shard_map/ppermute | solution.py:369
  30.7 0.0 copy-done.4
  30.7 4.4 %shard_map.104 = (f32[8,2048]{1,0:T(8,128)S(1)}, f32[8,2048]{1,0:T(8,128)S(1)}, f32[8,2048]{1,0:T(8,128)S(1)}, f32[8,2048]{1,0:T(8,128)S(1)}) custom-call(s32[4,64]{1,0:T(4,128)S(1)} %bitcast.2, f32[8,10240]{1,0:T(8,128)S(1)} %get-tuple-element.26.own, f32[8,10240]{1,0:T(8,128)S(1)} %collective-permute-done.2.arr1, ...), custom_call_target="tpu_custom_call" | custom-call | flops 5750000128 | tf_op jit(solution)/shard_map/pallas_call | solution.py:327
  35.1 0.3 collective-permute-start.5
  35.4 2.9 %collective-permute-start.6 = (f32[8,2048]{1,0:T(8,128)S(1)}, f32[8,2048]{1,0:T(8,128)S(1)}, u32[]{:S(2)}, u32[]{:S(2)}) collective-permute-start(f32[8,2048]{1,0:T(8,128)S(1)} %get-tuple-element.29), channel_id=1, source_target_pairs={{0,2},{1,3},{2,0},{3,1},{4,6},{5,7},{6,4},{7,5},{8,10},{9,11},{10,... | collective-permute-start | bytes 196616 | tf_op jit(solution)/shard_map/ppermute | solution.py:369
  38.3 2.4 %collective-permute-start.7 = (f32[8,2048]{1,0:T(8,128)S(1)}, f32[8,2048]{1,0:T(8,128)S(1)}, u32[]{:S(2)}, u32[]{:S(2)}) collective-permute-start(f32[8,2048]{1,0:T(8,128)S(1)} %get-tuple-element.30), channel_id=1, source_target_pairs={{0,1},{1,2},{2,3},{3,0},{4,5},{5,6},{6,7},{7,4},{8,9},{9,10},{10,1... | collective-permute-start | bytes 196616 | tf_op jit(solution)/shard_map/ppermute | solution.py:369
  40.7 0.0 all-to-all-done.packets
  40.7 0.0 copy-done.2
  40.7 0.0 copy-done.3
  40.7 4.9 %shard_map.103.far = f32[8,8192]{1,0:T(8,128)S(1)} custom-call(s32[62]{0:T(128)S(1)} %copy-done.2, s32[1,63]{1,0:T(1,128)S(1)} %copy-done.3, f32[32,4,128]{2,1,0:T(4,128)S(1)} %all-to-all-done.packets, f32[8,1152]{1,0:T(8,128)S(1)} %collective-permute-done.other.after, f32[31,8,128]{2,1,0:T(8,128)S(1)} %get-tuple-element.23.pairs, ...), custom_call_target="tpu_custom_call" | custom-call | tf_op jit(solution)/shard_map/pallas_call | solution.py:327
  45.6 0.0 collective-permute-done.5.near1
  45.6 0.0 collective-permute-done.6.near2
  45.6 0.0 collective-permute-done.7.near3
  45.7 1.4 %shard_map.105 = f32[8,8192]{1,0:T(8,128)} custom-call(s32[64,128]{1,0:T(8,128)S(1)} %get-tuple-element.18.inverse, f32[8,8192]{1,0:T(8,128)S(1)} %shard_map.103.far, f32[8,2048]{1,0:T(8,128)S(1)} %get-tuple-element.27.near0, f32[8,2048]{1,0:T(8,128)S(1)} %collective-permute-done.5.near1, f32[8,2048]{1,0:T(8,128)S(1)} %collective-permute-done.6.near2, ...), custom_call_target="tpu_custom_call" | custom-call | tf_op jit(solution)/shard_map/pallas_call | solution.py:327
Async XLA Ops:
  0.0 0.9 %copy-start = (f32[8,8192]{1,0:T(8,128)S(1)}, f32[8,8192]{1,0:T(8,128)}, u32[]{:S(2)}) copy-start(f32[8,8192]{1,0:T(8,128)} %panels_hbm.1) | copy-start | bytes 786436
  1.0 0.8 %copy-start.1 = (s32[64,128]{1,0:T(8,128)S(1)}, s32[64,128]{1,0:T(8,128)}, u32[]{:S(2)}) copy-start(s32[64,128]{1,0:T(8,128)} %order_hbm.1) | copy-start | bytes 98308
  5.1 5.3 %collective-permute-start = (f32[8,1152]{1,0:T(8,128)S(1)}, f32[8,1152]{1,0:T(8,128)S(1)}, u32[]{:S(2)}, u32[]{:S(2)}) collective-permute-start(f32[8,1152]{1,0:T(8,128)S(1)} %get-tuple-element.20.packet), channel_id=1, source_target_pairs={{0,4},{4,0},{8,12},{12,8},{16,20},{20,16},{24,28},{28,24},{32,36},... | collective-permute-start | bytes 110600 | tf_op jit(solution)/shard_map/ppermute | solution.py:401
  5.2 5.2 %collective-permute-start.1 = (f32[8,1024]{1,0:T(8,128)S(1)}, f32[8,1024]{1,0:T(8,128)S(1)}, u32[]{:S(2)}, u32[]{:S(2)}) collective-permute-start(f32[8,1024]{1,0:T(8,128)S(1)} %get-tuple-element.21), channel_id=1, source_target_pairs={{4,8},{12,16},{20,24},{28,32},{36,40},{44,48},{52,56},{60,64},{68,... | collective-permute-start | bytes 98312 | tf_op jit(solution)/shard_map/ppermute | solution.py:400
  11.2 16.9 %collective-permute-start.4 = (f32[8,10240]{1,0:T(8,128)S(1)}, f32[8,10240]{1,0:T(8,128)S(1)}, u32[]{:S(2)}, u32[]{:S(2)}) collective-permute-start(f32[8,10240]{1,0:T(8,128)S(1)} %get-tuple-element.26.own), channel_id=1, source_target_pairs={{0,3},{1,0},{2,1},{3,2},{4,7},{5,4},{6,5},{7,6},{8,11},{9,8},{10,9... | collective-permute-start | bytes 983048 | tf_op jit(solution)/shard_map/ppermute | solution.py:369
  11.6 16.5 %collective-permute-start.3 = (f32[8,10240]{1,0:T(8,128)S(1)}, f32[8,10240]{1,0:T(8,128)S(1)}, u32[]{:S(2)}, u32[]{:S(2)}) collective-permute-start(f32[8,10240]{1,0:T(8,128)S(1)} %get-tuple-element.26.own), channel_id=1, source_target_pairs={{0,2},{1,3},{2,0},{3,1},{4,6},{5,7},{6,4},{7,5},{8,10},{9,11},{10,... | collective-permute-start | bytes 983048 | tf_op jit(solution)/shard_map/ppermute | solution.py:369
  14.5 16.2 %collective-permute-start.2 = (f32[8,10240]{1,0:T(8,128)S(1)}, f32[8,10240]{1,0:T(8,128)S(1)}, u32[]{:S(2)}, u32[]{:S(2)}) collective-permute-start(f32[8,10240]{1,0:T(8,128)S(1)} %get-tuple-element.26.own), channel_id=1, source_target_pairs={{0,1},{1,2},{2,3},{3,0},{4,5},{5,6},{6,7},{7,4},{8,9},{9,10},{10,1... | collective-permute-start | bytes 983048 | tf_op jit(solution)/shard_map/ppermute | solution.py:369
  14.5 26.2 %all-to-all-start = ((f32[32,4,128]{2,1,0:T(4,128)}), f32[32,4,128]{2,1,0:T(4,128)S(1)}, u32[]{:S(2)}, u32[]{:S(2)}) async-start(f32[32,4,128]{2,1,0:T(4,128)} %get-tuple-element.22), calls=%async_computation | async-start | bytes 131072 | tf_op jit(solution)/shard_map/all_to_all | solution.py:412
  26.0 4.7 %copy-start.4 = (s32[64,4]{0,1:T(4,128)S(1)}, s32[64,4]{0,1:T(4,128)}, u32[]{:S(2)}) copy-start(s32[64,4]{0,1:T(4,128)} %param.12) | copy-start | bytes 3076
  28.1 12.6 %copy-start.2 = (s32[62]{0:T(128)S(1)}, s32[62]{0:T(128)}, u32[]{:S(2)}) copy-start(s32[62]{0:T(128)} %cross_flags.1) | copy-start | bytes 748
  28.1 12.6 %copy-start.3 = (s32[1,63]{1,0:T(1,128)S(1)}, s32[1,63]{1,0:T(1,128)}, u32[]{:S(2)}) copy-start(s32[1,63]{1,0:T(1,128)} %flags.1) | copy-start | bytes 760
  35.1 10.6 %collective-permute-start.5 = (f32[8,2048]{1,0:T(8,128)S(1)}, f32[8,2048]{1,0:T(8,128)S(1)}, u32[]{:S(2)}, u32[]{:S(2)}) collective-permute-start(f32[8,2048]{1,0:T(8,128)S(1)} %get-tuple-element.28), channel_id=1, source_target_pairs={{0,3},{1,0},{2,1},{3,2},{4,7},{5,4},{6,5},{7,6},{8,11},{9,8},{10,9... | collective-permute-start | bytes 196616 | tf_op jit(solution)/shard_map/ppermute | solution.py:369
  35.4 10.2 %collective-permute-start.6 = (f32[8,2048]{1,0:T(8,128)S(1)}, f32[8,2048]{1,0:T(8,128)S(1)}, u32[]{:S(2)}, u32[]{:S(2)}) collective-permute-start(f32[8,2048]{1,0:T(8,128)S(1)} %get-tuple-element.29), channel_id=1, source_target_pairs={{0,2},{1,3},{2,0},{3,1},{4,6},{5,7},{6,4},{7,5},{8,10},{9,11},{10,... | collective-permute-start | bytes 196616 | tf_op jit(solution)/shard_map/ppermute | solution.py:369
  38.3 7.4 %collective-permute-start.7 = (f32[8,2048]{1,0:T(8,128)S(1)}, f32[8,2048]{1,0:T(8,128)S(1)}, u32[]{:S(2)}, u32[]{:S(2)}) collective-permute-start(f32[8,2048]{1,0:T(8,128)S(1)} %get-tuple-element.30), channel_id=1, source_target_pairs={{0,1},{1,2},{2,3},{3,0},{4,5},{5,6},{6,7},{7,4},{8,9},{9,10},{10,1... | collective-permute-start | bytes 196616 | tf_op jit(solution)/shard_map/ppermute | solution.py:369

commit v5 on v4

--- a/solution.py
+++ b/solution.py
@@ -186,8 +186,7 @@
     packets[...] = jnp.broadcast_to(rows[None], packets.shape)
 
 
-def near_kernel(cols, own, arr1, arr2, arr3, tiles_hbm, out0, out1, out2, out3, held, tiles, sems):
-    copies = chunked(tiles_hbm, tiles, sems, 4)
+def near_kernel(cols, own, arr1, arr2, arr3, tiles, out0, out1, out2, out3, held):
     leaves = tiles.shape[0]
     slots = tiles.shape[1]
     base = lax.axis_index("leaf") * leaves - W
@@ -221,7 +220,6 @@
 
     quarter = leaves // 16
     for c in range(4):
-        copies[c].wait()
         lax.fori_loop(c * quarter, (c + 1) * quarter, group, 0, unroll=UNROLL)
 
 
@@ -429,15 +427,13 @@
         cols, path = lax.optimization_barrier((cols, path))
     near = call(
         near_kernel,
-        "svvvvh",
+        "svvvvv",
         (cols, own, *others, near_tiles),
         [((rhs, leaves * near_tiles.shape[2]), F32)] * 4,
         [
             pltpu.VMEM((leaves + 2 * W, 2 * parts * rhs, size), BF16),
-            pltpu.VMEM(near_tiles.shape, F32),
-            dma((4,)),
         ],
-        0,
+        46,
         NEAR_US,
     )
     back = [near[0]] + [turned(near[k], -k) for k in (1, 2, 3)]

time: 47.4 us -> 45.3 us (0.956)
  the two profiles are of different devices: /device:TPU:114 before, /device:TPU:8 now
where the time goes in v5:
time: 45.3 us; the launch traced here: 45 us
  starting transfers between devices  26.2 us (58%)
  Pallas kernels  14.9 us (33%)
  waiting for transfers between devices  2.01 us (4%)
  local copies, waits for them, and re-layouts  1.79 us (4%)
    all_to_all x1, starting transfers between devices, local(): gathered = lax.all_to_all(packets, 'leaf', 0, 0, axis_index_groups=groups)  16.6 us
    pallas_call x6, Pallas kernels, call(): pl.pallas_call(kernel, out_shape=[jax.ShapeDtypeStruct(s, t) for s, t in...  14.9 us
    ppermute x6, starting transfers between devices, turned(): return lax.ppermute(x, 'vec', [(i, (i + k) % parts) for i in range(parts)])  8.86 us
    unnamed x12, local copies, waits for them, and re-layouts  1.79 us
    all_to_all x1, waiting for transfers between devices, local(): gathered = lax.all_to_all(packets, 'leaf', 0, 0, axis_index_groups=groups)  1.47 us
  transfers between devices with their start and end apart: 9, of which 2 were waited for; matrix products, arithmetic and copies ran while one was open for 0% of the time, Pallas kernels for 21%

profile of v5, /device:TPU:8, one launch (start us, length us, event | category | flops | bytes accessed | tf_op | source)
XLA Modules:
  0.0 45.0 jit_solution(8876092122880797129)
XLA Ops:
  0.0 0.0 copy-start
  0.0 0.9 %copy-done = f32[8,8192]{1,0:T(8,128)S(1)} copy-done((f32[8,8192]{1,0:T(8,128)S(1)}, f32[8,8192]{1,0:T(8,128)}, u32[]{:S(2)}) %copy-start) | copy-done | bytes 262168
  1.0 0.0 copy-start.1
  1.0 0.8 %copy-done.1 = s32[64,128]{1,0:T(8,128)S(1)} copy-done((s32[64,128]{1,0:T(8,128)S(1)}, s32[64,128]{1,0:T(8,128)}, u32[]{:S(2)}) %copy-start.1) | copy-done | bytes 32792
  1.7 3.4 %shard_map.100 = (f32[8,10240]{1,0:T(8,128)S(1)}, f32[8,1024]{1,0:T(8,128)S(1)}, f32[31,8,128]{2,1,0:T(8,128)S(1)}, f32[8,1152]{1,0:T(8,128)S(1)}, s32[64,128]{1,0:T(8,128)S(1)}) custom-call(f32[8,8192]{1,0:T(8,128)S(1)} %copy-done, s32[64,128]{1,0:T(8,128)S(1)} %copy-done.1, f32[64,64,128]{2,1,0:T(8,128)} %basis_hbm.3, f32[63,64,128]{2,1,0:T(8,128)} %bitcast.3), custom_call_target="tpu_custom_call" | custom-call | tf_op jit(solution)/shard_map/pallas_call | solution.py:325
  5.1 0.1 collective-permute-start
  5.2 0.7 %collective-permute-start.1 = (f32[8,1024]{1,0:T(8,128)S(1)}, f32[8,1024]{1,0:T(8,128)S(1)}, u32[]{:S(2)}, u32[]{:S(2)}) collective-permute-start(f32[8,1024]{1,0:T(8,128)S(1)} %get-tuple-element.21), channel_id=1, source_target_pairs={{4,8},{12,16},{20,24},{28,32},{36,40},{44,48},{52,56},{60,64},{68,... | collective-permute-start | bytes 98312 | tf_op jit(solution)/shard_map/ppermute | solution.py:398
  5.9 0.0 collective-permute-done.1.far_rim
  5.9 0.5 %collective-permute-done.other.after = f32[8,1152]{1,0:T(8,128)S(1)} collective-permute-done((f32[8,1152]{1,0:T(8,128)S(1)}, f32[8,1152]{1,0:T(8,128)S(1)}, u32[]{:S(2)}, u32[]{:S(2)}) %collective-permute-start) | collective-permute-done | bytes 36896 | tf_op jit(solution)/shard_map/ppermute | solution.py:399
  6.4 0.7 %shard_map.101 = (f32[8,10240]{1,0:T(8,128)S(1)}, f32[32,4,128]{2,1,0:T(4,128)}) custom-call(f32[8,10240]{1,0:T(8,128)S(1)} %get-tuple-element.19.middle, f32[8,1152]{1,0:T(8,128)S(1)} %get-tuple-element.20.packet, f32[8,1152]{1,0:T(8,128)S(1)} %collective-permute-done.other.after, ...), custom_call_target="tpu_custom_call", output_to_operand_aliasing={{0}: (0, {})} | custom-call | tf_op jit(solution)/shard_map/pallas_call | solution.py:325
  7.1 2.2 %collective-permute-start.4 = (f32[8,10240]{1,0:T(8,128)S(1)}, f32[8,10240]{1,0:T(8,128)S(1)}, u32[]{:S(2)}, u32[]{:S(2)}) collective-permute-start(f32[8,10240]{1,0:T(8,128)S(1)} %get-tuple-element.26.own), channel_id=1, source_target_pairs={{0,3},{1,0},{2,1},{3,2},{4,7},{5,4},{6,5},{7,6},{8,11},{9,8},{10,9... | collective-permute-start | bytes 983048 | tf_op jit(solution)/shard_map/ppermute | solution.py:367
  9.3 0.9 %collective-permute-start.3 = (f32[8,10240]{1,0:T(8,128)S(1)}, f32[8,10240]{1,0:T(8,128)S(1)}, u32[]{:S(2)}, u32[]{:S(2)}) collective-permute-start(f32[8,10240]{1,0:T(8,128)S(1)} %get-tuple-element.26.own), channel_id=1, source_target_pairs={{0,2},{1,3},{2,0},{3,1},{4,6},{5,7},{6,4},{7,5},{8,10},{9,11},{10,... | collective-permute-start | bytes 983048 | tf_op jit(solution)/shard_map/ppermute | solution.py:367
  10.2 1.9 %collective-permute-start.2 = (f32[8,10240]{1,0:T(8,128)S(1)}, f32[8,10240]{1,0:T(8,128)S(1)}, u32[]{:S(2)}, u32[]{:S(2)}) collective-permute-start(f32[8,10240]{1,0:T(8,128)S(1)} %get-tuple-element.26.own), channel_id=1, source_target_pairs={{0,1},{1,2},{2,3},{3,0},{4,5},{5,6},{6,7},{7,4},{8,9},{9,10},{10,1... | collective-permute-start | bytes 983048 | tf_op jit(solution)/shard_map/ppermute | solution.py:367
  12.0 16.6 %all-to-all-start = ((f32[32,4,128]{2,1,0:T(4,128)}), f32[32,4,128]{2,1,0:T(4,128)S(1)}, u32[]{:S(2)}, u32[]{:S(2)}) async-start(f32[32,4,128]{2,1,0:T(4,128)} %get-tuple-element.22), calls=%async_computation | async-start | bytes 131072 | tf_op jit(solution)/shard_map/all_to_all | solution.py:410
  28.6 0.0 copy-start.4
  28.6 0.0 copy-start.5
  28.6 2.2 %shard_map.102.path = f32[3,64,128]{2,1,0:T(8,128)S(1)} custom-call(f32[8,1152]{1,0:T(8,128)S(1)} %collective-permute-done.other.after, f32[63,64,128]{2,1,0:T(8,128)} %bitcast.4, f32[62,64,64]{2,1,0:T(8,128)} %coupling_hbm.1, f32[60,64,64]{2,1,0:T(8,128)} %transfer_hbm.3), custom_call_target="tpu_custom_call" | custom-call | tf_op jit(solution)/shard_map/pallas_call | solution.py:325
  30.8 0.0 copy-start.2
  30.9 0.0 copy-start.3
  30.9 0.0 collective-permute-done.4.arr3
  30.9 0.0 collective-permute-done.3.arr2
  30.9 0.0 collective-permute-done.2.arr1
  30.9 0.1 copy-done.4
  31.0 0.0 copy-done.5
  31.0 2.3 %shard_map.104 = (f32[8,2048]{1,0:T(8,128)S(1)}, f32[8,2048]{1,0:T(8,128)S(1)}, f32[8,2048]{1,0:T(8,128)S(1)}, f32[8,2048]{1,0:T(8,128)S(1)}) custom-call(s32[4,64]{1,0:T(4,128)S(1)} %bitcast.2, f32[8,10240]{1,0:T(8,128)S(1)} %get-tuple-element.26.own, f32[8,10240]{1,0:T(8,128)S(1)} %collective-permute-done.2.arr1, ...), custom_call_target="tpu_custom_call" | custom-call | flops 5750000128 | tf_op jit(solution)/shard_map/pallas_call | solution.py:325
  33.2 0.2 collective-permute-start.5
  33.4 1.3 %collective-permute-start.6 = (f32[8,2048]{1,0:T(8,128)S(1)}, f32[8,2048]{1,0:T(8,128)S(1)}, u32[]{:S(2)}, u32[]{:S(2)}) collective-permute-start(f32[8,2048]{1,0:T(8,128)S(1)} %get-tuple-element.29), channel_id=1, source_target_pairs={{0,2},{1,3},{2,0},{3,1},{4,6},{5,7},{6,4},{7,5},{8,10},{9,11},{10,... | collective-permute-start | bytes 196616 | tf_op jit(solution)/shard_map/ppermute | solution.py:367
  34.7 2.4 %collective-permute-start.7 = (f32[8,2048]{1,0:T(8,128)S(1)}, f32[8,2048]{1,0:T(8,128)S(1)}, u32[]{:S(2)}, u32[]{:S(2)}) collective-permute-start(f32[8,2048]{1,0:T(8,128)S(1)} %get-tuple-element.30), channel_id=1, source_target_pairs={{0,1},{1,2},{2,3},{3,0},{4,5},{5,6},{6,7},{7,4},{8,9},{9,10},{10,1... | collective-permute-start | bytes 196616 | tf_op jit(solution)/shard_map/ppermute | solution.py:367
  37.2 1.5 %all-to-all-done.packets = f32[32,4,128]{2,1,0:T(4,128)S(1)} async-done(((f32[32,4,128]{2,1,0:T(4,128)}), f32[32,4,128]{2,1,0:T(4,128)S(1)}, u32[]{:S(2)}, u32[]{:S(2)}) %all-to-all-start) | async-done | bytes 65568 | tf_op jit(solution)/shard_map/all_to_all | solution.py:410
  38.6 0.0 copy-done.2
  38.6 0.0 copy-done.3
  38.6 4.9 %shard_map.103.far = f32[8,8192]{1,0:T(8,128)S(1)} custom-call(s32[62]{0:T(128)S(1)} %copy-done.2, s32[1,63]{1,0:T(1,128)S(1)} %copy-done.3, f32[32,4,128]{2,1,0:T(4,128)S(1)} %all-to-all-done.packets, f32[8,1152]{1,0:T(8,128)S(1)} %collective-permute-done.other.after, f32[31,8,128]{2,1,0:T(8,128)S(1)} %get-tuple-element.23.pairs, ...), custom_call_target="tpu_custom_call" | custom-call | tf_op jit(solution)/shard_map/pallas_call | solution.py:325
  43.6 0.0 collective-permute-done.5.near1
  43.6 0.0 collective-permute-done.6.near2
  43.6 0.0 collective-permute-done.7.near3
  43.6 1.4 %shard_map.105 = f32[8,8192]{1,0:T(8,128)} custom-call(s32[64,128]{1,0:T(8,128)S(1)} %get-tuple-element.18.inverse, f32[8,8192]{1,0:T(8,128)S(1)} %shard_map.103.far, f32[8,2048]{1,0:T(8,128)S(1)} %get-tuple-element.27.near0, f32[8,2048]{1,0:T(8,128)S(1)} %collective-permute-done.5.near1, f32[8,2048]{1,0:T(8,128)S(1)} %collective-permute-done.6.near2, ...), custom_call_target="tpu_custom_call" | custom-call | tf_op jit(solution)/shard_map/pallas_call | solution.py:325
Async XLA Ops:
  0.0 0.9 %copy-start = (f32[8,8192]{1,0:T(8,128)S(1)}, f32[8,8192]{1,0:T(8,128)}, u32[]{:S(2)}) copy-start(f32[8,8192]{1,0:T(8,128)} %panels_hbm.1) | copy-start | bytes 786436
  1.0 0.8 %copy-start.1 = (s32[64,128]{1,0:T(8,128)S(1)}, s32[64,128]{1,0:T(8,128)}, u32[]{:S(2)}) copy-start(s32[64,128]{1,0:T(8,128)} %order_hbm.1) | copy-start | bytes 98308
  5.1 1.3 %collective-permute-start = (f32[8,1152]{1,0:T(8,128)S(1)}, f32[8,1152]{1,0:T(8,128)S(1)}, u32[]{:S(2)}, u32[]{:S(2)}) collective-permute-start(f32[8,1152]{1,0:T(8,128)S(1)} %get-tuple-element.20.packet), channel_id=1, source_target_pairs={{0,4},{4,0},{8,12},{12,8},{16,20},{20,16},{24,28},{28,24},{32,36},... | collective-permute-start | bytes 110600 | tf_op jit(solution)/shard_map/ppermute | solution.py:399
  5.2 0.7 %collective-permute-start.1 = (f32[8,1024]{1,0:T(8,128)S(1)}, f32[8,1024]{1,0:T(8,128)S(1)}, u32[]{:S(2)}, u32[]{:S(2)}) collective-permute-start(f32[8,1024]{1,0:T(8,128)S(1)} %get-tuple-element.21), channel_id=1, source_target_pairs={{4,8},{12,16},{20,24},{28,32},{36,40},{44,48},{52,56},{60,64},{68,... | collective-permute-start | bytes 98312 | tf_op jit(solution)/shard_map/ppermute | solution.py:398
  7.1 23.8 %collective-permute-start.4 = (f32[8,10240]{1,0:T(8,128)S(1)}, f32[8,10240]{1,0:T(8,128)S(1)}, u32[]{:S(2)}, u32[]{:S(2)}) collective-permute-start(f32[8,10240]{1,0:T(8,128)S(1)} %get-tuple-element.26.own), channel_id=1, source_target_pairs={{0,3},{1,0},{2,1},{3,2},{4,7},{5,4},{6,5},{7,6},{8,11},{9,8},{10,9... | collective-permute-start | bytes 983048 | tf_op jit(solution)/shard_map/ppermute | solution.py:367
  9.3 21.6 %collective-permute-start.3 = (f32[8,10240]{1,0:T(8,128)S(1)}, f32[8,10240]{1,0:T(8,128)S(1)}, u32[]{:S(2)}, u32[]{:S(2)}) collective-permute-start(f32[8,10240]{1,0:T(8,128)S(1)} %get-tuple-element.26.own), channel_id=1, source_target_pairs={{0,2},{1,3},{2,0},{3,1},{4,6},{5,7},{6,4},{7,5},{8,10},{9,11},{10,... | collective-permute-start | bytes 983048 | tf_op jit(solution)/shard_map/ppermute | solution.py:367
  10.2 20.7 %collective-permute-start.2 = (f32[8,10240]{1,0:T(8,128)S(1)}, f32[8,10240]{1,0:T(8,128)S(1)}, u32[]{:S(2)}, u32[]{:S(2)}) collective-permute-start(f32[8,10240]{1,0:T(8,128)S(1)} %get-tuple-element.26.own), channel_id=1, source_target_pairs={{0,1},{1,2},{2,3},{3,0},{4,5},{5,6},{6,7},{7,4},{8,9},{9,10},{10,1... | collective-permute-start | bytes 983048 | tf_op jit(solution)/shard_map/ppermute | solution.py:367
  12.0 26.6 %all-to-all-start = ((f32[32,4,128]{2,1,0:T(4,128)}), f32[32,4,128]{2,1,0:T(4,128)S(1)}, u32[]{:S(2)}, u32[]{:S(2)}) async-start(f32[32,4,128]{2,1,0:T(4,128)} %get-tuple-element.22), calls=%async_computation | async-start | bytes 131072 | tf_op jit(solution)/shard_map/all_to_all | solution.py:410
  28.6 2.3 %copy-start.4 = (f32[64,4,32,128]{3,2,1,0:T(8,128)S(1)}, f32[64,4,32,128]{3,2,1,0:T(8,128)}, u32[]{:S(2)}) copy-start(f32[64,4,32,128]{3,2,1,0:T(8,128)} %tiles.1) | copy-start | bytes 12582916
  28.6 2.3 %copy-start.5 = (s32[64,4]{0,1:T(4,128)S(1)}, s32[64,4]{0,1:T(4,128)}, u32[]{:S(2)}) copy-start(s32[64,4]{0,1:T(4,128)} %param.12) | copy-start | bytes 3076
  30.8 7.8 %copy-start.2 = (s32[62]{0:T(128)S(1)}, s32[62]{0:T(128)}, u32[]{:S(2)}) copy-start(s32[62]{0:T(128)} %cross_flags.1) | copy-start | bytes 748
  30.9 7.8 %copy-start.3 = (s32[1,63]{1,0:T(1,128)S(1)}, s32[1,63]{1,0:T(1,128)}, u32[]{:S(2)}) copy-start(s32[1,63]{1,0:T(1,128)} %flags.1) | copy-start | bytes 760
  33.2 10.3 %collective-permute-start.5 = (f32[8,2048]{1,0:T(8,128)S(1)}, f32[8,2048]{1,0:T(8,128)S(1)}, u32[]{:S(2)}, u32[]{:S(2)}) collective-permute-start(f32[8,2048]{1,0:T(8,128)S(1)} %get-tuple-element.28), channel_id=1, source_target_pairs={{0,3},{1,0},{2,1},{3,2},{4,7},{5,4},{6,5},{7,6},{8,11},{9,8},{10,9... | collective-permute-start | bytes 196616 | tf_op jit(solution)/shard_map/ppermute | solution.py:367
  33.4 10.2 %collective-permute-start.6 = (f32[8,2048]{1,0:T(8,128)S(1)}, f32[8,2048]{1,0:T(8,128)S(1)}, u32[]{:S(2)}, u32[]{:S(2)}) collective-permute-start(f32[8,2048]{1,0:T(8,128)S(1)} %get-tuple-element.29), channel_id=1, source_target_pairs={{0,2},{1,3},{2,0},{3,1},{4,6},{5,7},{6,4},{7,5},{8,10},{9,11},{10,... | collective-permute-start | bytes 196616 | tf_op jit(solution)/shard_map/ppermute | solution.py:367
  34.7 8.8 %collective-permute-start.7 = (f32[8,2048]{1,0:T(8,128)S(1)}, f32[8,2048]{1,0:T(8,128)S(1)}, u32[]{:S(2)}, u32[]{:S(2)}) collective-permute-start(f32[8,2048]{1,0:T(8,128)S(1)} %get-tuple-element.30), channel_id=1, source_target_pairs={{0,1},{1,2},{2,3},{3,0},{4,5},{5,6},{6,7},{7,4},{8,9},{9,10},{10,1... | collective-permute-start | bytes 196616 | tf_op jit(solution)/shard_map/ppermute | solution.py:367
